TPU v7x, 256 devices: a whole 4x4x8 slice. The times are simulated.
256 devices in a mesh: pair: 16 (over x, z_lo, core), pw: 16 (over z_hi, y).
Axes of the slice: x: 4, y: 4, z: 8 (z_hi: 4, z_lo: 2; z = z_hi * 2 + z_lo), core: 2. Of those that a mesh axis runs over, the one named last changes fastest.
Arguments:
- pair_products: bfloat16 [32768, 8192], P('pw', 'pair'), may hold values from -40 to 40
- basis: bfloat16 [32768, 1024], P('pw'), may hold values from -0.046875 to 0.046875
- val_energy: float32 [128], replicated, may hold values from -0.05 to -0.001
- cond_energy: float32 [128], replicated, may hold values from 0.001 to 40
- frequencies: float32 [8], replicated, may hold values from 0.002 to 20
- valence_index: int32 [8192], P('pair'), may hold values from 0 to 127
- conduction_index: int32 [8192], P('pair'), may hold values from 0 to 127
Outputs:
- response: float32 [8, 1024, 1024], P(None, 'pw', 'pair')
All inputs are finite; a program needn't handle non-finite values.
Results may differ from a plain program's by a relative error of at most 0.0055.
Values may be sent and summed in bfloat16 or wider, within the bound.
A program may use at most 64 MiB of HBM per device.

v0:
```python
import jax
import jax.numpy as jnp
from jax import lax
from jax.sharding import PartitionSpec as P

GROUPS = 2


def in_blocks(x, dim, count):
    before, after = (x.shape[:dim], x.shape[dim + 1 :])
    return jnp.moveaxis(x.reshape(*before, count, -1, *after), dim, 0)


def sent_and_summed(x, axis, dim):
    blocks = in_blocks(x, dim, lax.axis_size(axis))
    arrived = lax.all_to_all(blocks, axis, split_axis=0, concat_axis=0, tiled=True)
    return arrived.sum(axis=0)


def in_order(blocks, dim):
    lengths = list(blocks.shape[1:])
    lengths[dim] *= blocks.shape[0]
    return jnp.moveaxis(blocks, 0, dim).reshape(lengths)


def from_everyone(x, axis):
    copies = jnp.broadcast_to(x, (lax.axis_size(axis), *x.shape))
    return lax.all_to_all(copies, axis, split_axis=0, concat_axis=0, tiled=True)


def gathered_copies(x, axis, dim):
    return in_order(from_everyone(x, axis), dim)


def sent_and_summed_2(x, axis, dim):
    count = lax.axis_size(axis)
    blocks = lax.all_to_all(in_blocks(x, dim, count), axis, 0, 0, tiled=True)
    return jnp.sum(blocks.astype(jnp.float32), axis=0)


def lookup(index_array, table):
    levels = lax.broadcasted_iota(jnp.int32, (index_array.shape[0], table.shape[0]), 1)
    return jnp.sum(jnp.where(index_array[:, None] == levels, table[None, :], 0.0), axis=1)


def make_weights(
    valence_index, conduction_index, val_energy, cond_energy, frequencies, pairs_total
):
    energy_gap = lookup(conduction_index, cond_energy) - lookup(valence_index, val_energy)
    return (
        -4.0
        * energy_gap[None, :]
        / (energy_gap[None, :] ** 2 + frequencies[:, None] ** 2)
        / pairs_total
    )


def scaled(weight_block, own_rows):
    return (weight_block[:, None, :] * own_rows.astype(jnp.float32)[None]).astype(jnp.bfloat16)


def per_device(
    pair_products, basis, val_energy, cond_energy, frequencies, valence_index, conduction_index
):
    rows_local = pair_products.shape[1]
    pairs_total = rows_local * lax.axis_size("pair")
    block_size = rows_local // GROUPS
    weights = make_weights(
        valence_index, conduction_index, val_energy, cond_energy, frequencies, pairs_total
    )
    gram_total = None
    kept_rows = []
    for group in range(GROUPS):
        pair_block = pair_products[:, group * block_size : (group + 1) * block_size]
        weight_block = weights[:, group * block_size : (group + 1) * block_size]
        gram_rows = None
        own_rows = sent_and_summed(
            lax.dot_general(
                basis, pair_block, (((0,), (0,)), ((), ())), preferred_element_type=jnp.float32
            ),
            "pw",
            0,
        ).astype(jnp.bfloat16)
        weighted = scaled(weight_block, own_rows)
        gram_rows = jnp.einsum(
            "kpc,nc->kpn",
            weighted,
            gathered_copies(own_rows, "pw", 0),
            preferred_element_type=jnp.float32,
        )
        kept_rows.append(own_rows)
        summed_part = sent_and_summed_2(gram_rows.astype(jnp.bfloat16), "pair", 2)
        gram_total = summed_part if gram_total is None else gram_total + summed_part
    return gram_total


def solution(mesh):
    placed = (P("pw", "pair"), P("pw", None), P(), P(), P(), P("pair"), P("pair"))
    return jax.shard_map(
        per_device, mesh=mesh, in_specs=placed, out_specs=P(None, "pw", "pair"), check_vma=False
    )
```

profile of v0, /device:TPU:1, one launch (start us, length us, event | category | flops | bytes accessed | tf_op | source)
XLA Modules:
  0.0 168.9 jit_solution(187163185010513554)
XLA Ops:
  0.0 4.8 %fusion = f32[1024,256]{1,0:T(8,128)} fusion(bf16[2048,1024]{1,0:T(8,128)(2,1)} %param.8, bf16[2048,512]{1,0:T(8,128)(2,1)} %param.7), kind=kOutput, calls=%fused_computation.6 | convolution fusion | flops 1073741824 | bytes 6291456 | tf_op jit(solution)/shard_map/dot_general | solution.py:78
  4.8 11.8 %all-to-all-start.3 = ((f32[16,64,256]{2,1,0:T(8,128)}), f32[16,64,256]{2,1,0:T(8,128)S(1)}, u32[]{:S(2)}, u32[]{:S(2)}) async-start(f32[16,64,256]{2,1,0:T(8,128)} %bitcast.4), calls=%async_computation.3 | async-start | bytes 2097152 | tf_op jit(solution)/shard_map/all_to_all | solution.py:16
  16.5 4.7 %fusion.2 = f32[1024,256]{1,0:T(8,128)} fusion(bf16[2048,1024]{1,0:T(8,128)(2,1)} %param.8, bf16[2048,512]{1,0:T(8,128)(2,1)} %param.7), kind=kOutput, calls=%fused_computation.8 | convolution fusion | flops 1073741824 | bytes 6291456 | tf_op jit(solution)/shard_map/dot_general | solution.py:78
  21.3 20.6 %all-to-all-done.3 = f32[16,64,256]{2,1,0:T(8,128)S(1)} async-done(((f32[16,64,256]{2,1,0:T(8,128)}), f32[16,64,256]{2,1,0:T(8,128)S(1)}, u32[]{:S(2)}, u32[]{:S(2)}) %all-to-all-start.3) | async-done | bytes 1048608 | tf_op jit(solution)/shard_map/all_to_all | solution.py:16
  41.9 7.9 %all-to-all-start = ((f32[16,64,256]{2,1,0:T(8,128)}), f32[16,64,256]{2,1,0:T(8,128)S(1)}, u32[]{:S(2)}, u32[]{:S(2)}) async-start(f32[16,64,256]{2,1,0:T(8,128)} %bitcast), calls=%async_computation | async-start | bytes 2097152 | tf_op jit(solution)/shard_map/all_to_all | solution.py:16
  49.8 0.1 reduce_sum.58
  49.9 27.3 %all-to-all-done = f32[16,64,256]{2,1,0:T(8,128)S(1)} async-done(((f32[16,64,256]{2,1,0:T(8,128)}), f32[16,64,256]{2,1,0:T(8,128)S(1)}, u32[]{:S(2)}, u32[]{:S(2)}) %all-to-all-start) | async-done | bytes 1048608 | tf_op jit(solution)/shard_map/all_to_all | solution.py:16
  77.2 0.8 broadcast_in_dim.39
  78.1 6.5 %all-to-all-start.4 = ((bf16[16,64,256]{2,1,0:T(8,128)(2,1)}), bf16[16,64,256]{2,1,0:T(8,128)(2,1)S(1)}, u32[]{:S(2)}, u32[]{:S(2)}) async-start(bf16[16,64,256]{2,1,0:T(8,128)(2,1)} %broadcast_in_dim.39), calls=%async_computation.4 | async-start | bytes 1048576 | tf_op jit(solution)/shard_map/all_to_all | solution.py:28
  84.6 14.9 %all-to-all-done.4 = bf16[16,64,256]{2,1,0:T(8,128)(2,1)S(1)} async-done(((bf16[16,64,256]{2,1,0:T(8,128)(2,1)}), bf16[16,64,256]{2,1,0:T(8,128)(2,1)S(1)}, u32[]{:S(2)}, u32[]{:S(2)}) %all-to-all-start.4) | async-done | bytes 524320 | tf_op jit(solution)/shard_map/all_to_all | solution.py:28
  99.6 0.8 broadcast_in_dim.38
  100.4 4.2 %all-to-all-start.1 = ((bf16[16,64,256]{2,1,0:T(8,128)(2,1)}), bf16[16,64,256]{2,1,0:T(8,128)(2,1)}, u32[]{:S(2)}, u32[]{:S(2)}) async-start(bf16[16,64,256]{2,1,0:T(8,128)(2,1)} %broadcast_in_dim.38), calls=%async_computation.1 | async-start | bytes 1048576 | tf_op jit(solution)/shard_map/all_to_all | solution.py:28
  104.7 0.4 select_reduce_fusion
  105.1 0.1 divide_multiply_fusion
  105.2 0.5 convolution_convert_fusion
  105.7 1.3 reshape.52
  107.0 1.9 %copy.14 = bf16[8,64,16,64]{3,1,0,2:T(8,128)(2,1)} copy(bf16[8,64,16,64]{3,2,1,0:T(8,128)(2,1)S(1)} %reshape.52) | data formatting | bytes 2097152 | tf_op jit(solution)/shard_map/reshape | solution.py:11
  108.9 4.6 %reshape.57 = bf16[16,2,16384]{2,1,0:T(2,128)(2,1)} reshape(bf16[16,8,64,64]{3,2,1,0:T(8,128)(2,1)} %bitcast.18) | data formatting | bytes 2097152
  113.6 2.7 %all-to-all-done.1 = bf16[16,64,256]{2,1,0:T(8,128)(2,1)} async-done(((bf16[16,64,256]{2,1,0:T(8,128)(2,1)}), bf16[16,64,256]{2,1,0:T(8,128)(2,1)}, u32[]{:S(2)}, u32[]{:S(2)}) %all-to-all-start.1) | async-done | bytes 524320 | tf_op jit(solution)/shard_map/all_to_all | solution.py:28
  116.2 11.0 %all-to-all-start.5 = ((bf16[16,2,16384]{2,1,0:T(2,128)(2,1)}), bf16[16,2,16384]{2,1,0:T(2,128)(2,1)S(1)}, u32[]{:S(2)}, u32[]{:S(2)}) async-start(bf16[16,2,16384]{2,1,0:T(2,128)(2,1)} %reshape.57), calls=%async_computation.5 | async-start | bytes 2097152 | tf_op jit(solution)/shard_map/all_to_all | solution.py:37
  127.2 2.5 %convolution_convert_fusion.1 = bf16[8,64,1024]{2,1,0:T(8,128)(2,1)} fusion(bf16[1024,256,1]{1,0,2:T(8,128)(2,1)} %bitcast.2, f32[64,256]{1,0:T(8,128)S(1)} %convert_element_type.47, f32[8,256]{1,0:T(8,128)S(1)} %get-tuple-element.6), kind=kOutput, calls=%fused_computation.5 | convolution fusion | flops 269221888 | bytes 1646592 | tf_op jit(solution)/shard_map/kpc,nc->kpn/dot_general | solution.py:85
  129.7 2.9 %reshape.49 = bf16[8,64,16,64]{3,2,1,0:T(8,128)(2,1)S(1)} reshape(bf16[8,64,1024]{2,1,0:T(8,128)(2,1)} %convolution_convert_fusion.1) | data formatting | bytes 2097152 | tf_op jit(solution)/shard_map/reshape | solution.py:11
  132.6 1.9 %copy.15 = bf16[8,64,16,64]{3,1,0,2:T(8,128)(2,1)} copy(bf16[8,64,16,64]{3,2,1,0:T(8,128)(2,1)S(1)} %reshape.49) | data formatting | bytes 2097152 | tf_op jit(solution)/shard_map/reshape | solution.py:11
  134.5 4.7 %reshape.55 = bf16[16,2,16384]{2,1,0:T(2,128)(2,1)} reshape(bf16[16,8,64,64]{3,2,1,0:T(8,128)(2,1)} %bitcast.19) | data formatting | bytes 2097152
  139.2 3.8 %all-to-all-done.5 = bf16[16,2,16384]{2,1,0:T(2,128)(2,1)S(1)} async-done(((bf16[16,2,16384]{2,1,0:T(2,128)(2,1)}), bf16[16,2,16384]{2,1,0:T(2,128)(2,1)S(1)}, u32[]{:S(2)}, u32[]{:S(2)}) %all-to-all-start.5) | async-done | bytes 1048608 | tf_op jit(solution)/shard_map/all_to_all | solution.py:37
  143.0 4.9 %all-to-all-start.2 = ((bf16[16,2,16384]{2,1,0:T(2,128)(2,1)}), bf16[16,2,16384]{2,1,0:T(2,128)(2,1)}, u32[]{:S(2)}, u32[]{:S(2)}) async-start(bf16[16,2,16384]{2,1,0:T(2,128)(2,1)} %reshape.55), calls=%async_computation.2 | async-start | bytes 2097152 | tf_op jit(solution)/shard_map/all_to_all | solution.py:37
  147.9 1.3 reshape.58
  149.3 0.4 convert_reduce_fusion
  149.7 14.2 %all-to-all-done.2 = bf16[16,2,16384]{2,1,0:T(2,128)(2,1)} async-done(((bf16[16,2,16384]{2,1,0:T(2,128)(2,1)}), bf16[16,2,16384]{2,1,0:T(2,128)(2,1)}, u32[]{:S(2)}, u32[]{:S(2)}) %all-to-all-start.2) | async-done | bytes 1048608 | tf_op jit(solution)/shard_map/all_to_all | solution.py:37
  164.0 3.8 %reshape.56 = bf16[16,8,64,64]{3,2,1,0:T(8,128)(2,1)S(1)} reshape(bf16[16,2,16384]{2,1,0:T(2,128)(2,1)} %all-to-all-done.2) | data formatting | bytes 2097152
  167.7 0.4 convert_reduce_fusion.1
  168.2 0.7 add.19
  (16 shorter events, 0.1 us)
Async XLA Ops:
  4.8 37.1 %all-to-all-start.3 = ((f32[16,64,256]{2,1,0:T(8,128)}), f32[16,64,256]{2,1,0:T(8,128)S(1)}, u32[]{:S(2)}, u32[]{:S(2)}) async-start(f32[16,64,256]{2,1,0:T(8,128)} %bitcast.4), calls=%async_computation.3 | async-start | bytes 2097152 | tf_op jit(solution)/shard_map/all_to_all | solution.py:16
  41.9 35.3 %all-to-all-start = ((f32[16,64,256]{2,1,0:T(8,128)}), f32[16,64,256]{2,1,0:T(8,128)S(1)}, u32[]{:S(2)}, u32[]{:S(2)}) async-start(f32[16,64,256]{2,1,0:T(8,128)} %bitcast), calls=%async_computation | async-start | bytes 2097152 | tf_op jit(solution)/shard_map/all_to_all | solution.py:16
  49.9 54.8 %copy-start = (s32[512]{0:T(512)S(1)}, s32[512]{0:T(512)}, u32[]{:S(2)}) copy-start(s32[512]{0:T(512)} %param.12) | copy-start | bytes 6148
  49.9 54.8 %copy-start.1 = (s32[512]{0:T(512)S(1)}, s32[512]{0:T(512)}, u32[]{:S(2)}) copy-start(s32[512]{0:T(512)} %param.13) | copy-start | bytes 6148
  49.9 54.8 %copy-start.2 = (f32[128]{0:T(128)S(1)}, f32[128]{0:T(128)}, u32[]{:S(2)}) copy-start(f32[128]{0:T(128)} %param.9) | copy-start | bytes 1540
  49.9 54.8 %copy-start.3 = (f32[128]{0:T(128)S(1)}, f32[128]{0:T(128)}, u32[]{:S(2)}) copy-start(f32[128]{0:T(128)} %param.10) | copy-start | bytes 1540
  49.9 55.2 %copy-start.4 = (f32[8]{0:T(128)S(1)}, f32[8]{0:T(128)}, u32[]{:S(2)}) copy-start(f32[8]{0:T(128)} %param.11) | copy-start | bytes 100
  78.1 21.5 %all-to-all-start.4 = ((bf16[16,64,256]{2,1,0:T(8,128)(2,1)}), bf16[16,64,256]{2,1,0:T(8,128)(2,1)S(1)}, u32[]{:S(2)}, u32[]{:S(2)}) async-start(bf16[16,64,256]{2,1,0:T(8,128)(2,1)} %broadcast_in_dim.39), calls=%async_computation.4 | async-start | bytes 1048576 | tf_op jit(solution)/shard_map/all_to_all | solution.py:28
  100.4 15.8 %all-to-all-start.1 = ((bf16[16,64,256]{2,1,0:T(8,128)(2,1)}), bf16[16,64,256]{2,1,0:T(8,128)(2,1)}, u32[]{:S(2)}, u32[]{:S(2)}) async-start(bf16[16,64,256]{2,1,0:T(8,128)(2,1)} %broadcast_in_dim.38), calls=%async_computation.1 | async-start | bytes 1048576 | tf_op jit(solution)/shard_map/all_to_all | solution.py:28
  116.2 26.8 %all-to-all-start.5 = ((bf16[16,2,16384]{2,1,0:T(2,128)(2,1)}), bf16[16,2,16384]{2,1,0:T(2,128)(2,1)S(1)}, u32[]{:S(2)}, u32[]{:S(2)}) async-start(bf16[16,2,16384]{2,1,0:T(2,128)(2,1)} %reshape.57), calls=%async_computation.5 | async-start | bytes 2097152 | tf_op jit(solution)/shard_map/all_to_all | solution.py:37
  143.0 21.0 %all-to-all-start.2 = ((bf16[16,2,16384]{2,1,0:T(2,128)(2,1)}), bf16[16,2,16384]{2,1,0:T(2,128)(2,1)}, u32[]{:S(2)}, u32[]{:S(2)}) async-start(bf16[16,2,16384]{2,1,0:T(2,128)(2,1)} %reshape.55), calls=%async_computation.2 | async-start | bytes 2097152 | tf_op jit(solution)/shard_map/all_to_all | solution.py:37
where the time goes:
time: 170 us; the launch traced here: 169 us
  waiting for transfers between devices  83.6 us (49%)
  starting transfers between devices  46.2 us (27%)
  local copies, waits for them, and re-layouts  24.2 us (14%)
  matrix products  12.5 us (7%)
  other arithmetic  2.19 us (1%)
    all_to_all x2, waiting for transfers between devices, sent_and_summed(): lax.all_to_all(blocks, axis, split_axis=0, concat_axis=0, tiled=True)  47.9 us
    all_to_all x2, starting transfers between devices, sent_and_summed(): lax.all_to_all(blocks, axis, split_axis=0, concat_axis=0, tiled=True)  19.6 us
    all_to_all x2, waiting for transfers between devices, sent_and_summed_2(): blocks = lax.all_to_all(in_blocks(x, dim, count), axis, 0, 0, tiled=True)  18.1 us
    all_to_all x2, waiting for transfers between devices, from_everyone(): return lax.all_to_all(copies, axis, split_axis=0, concat_axis=0, tiled=True)  17.6 us
    all_to_all x2, starting transfers between devices, sent_and_summed_2(): blocks = lax.all_to_all(in_blocks(x, dim, count), axis, 0, 0, tiled=True)  15.9 us
    unnamed x14, local copies, waits for them, and re-layouts  14.4 us
    all_to_all x2, starting transfers between devices, from_everyone(): return lax.all_to_all(copies, axis, split_axis=0, concat_axis=0, tiled=True)  10.7 us
    dot_general x2, matrix products, per_device(): lax.dot_general(basis, pair_block, (((0,), (0,)), ((), ())), preferred_el...  9.52 us
  transfers between devices with their start and end apart: 6, of which 6 were waited for; matrix products, arithmetic and copies ran while one was open for 16% of the time, Pallas kernels for 0%

commit v1 on v0

v1 whole, which is shorter than its diff:
```python
import functools

import jax
import jax.numpy as jnp
from jax import lax
from jax.experimental import pallas as pl
from jax.experimental.pallas import tpu as pltpu
from jax.sharding import PartitionSpec as P

F32 = jnp.float32
BF16 = jnp.bfloat16
MESH = pl.DeviceIdType.MESH
CHUNKS = 4
HALVES = 2


def kernel(
    pairs_total,
    pp_hbm,
    basis_hbm,
    val_ref,
    cond_ref,
    freq_ref,
    vidx_ref,
    cidx_ref,
    out_ref,
    basis_v,
    pp_v,
    psend,
    yrecv,
    zsend,
    zrecv,
    mbuf,
    nbuf,
    wbuf,
    acc,
    csend,
    crecv,
    basis_sem,
    pp_sem,
    y_ss,
    y_rs,
    z_ss,
    z_rs,
    m_ss,
    m_rs,
    n_ss,
    n_rs,
    r_ss,
    r_rs,
    w_ss,
    w_rs,
    c_ss,
    c_rs,
):
    pair, pw = lax.axis_index("pair"), lax.axis_index("pw")
    x, zl, cc = pair // 4, (pair // 2) % 2, pair % 2
    zh, y = pw // 4, pw % 4
    y_hi, y_lo = y // 2, y % 2

    def dev(x=x, zl=zl, cc=cc, zh=zh, y=y):
        return {"pair": x * 4 + zl * 2 + cc, "pw": zh * 4 + y}

    def basis_load(zb):
        return pltpu.make_async_copy(
            basis_hbm.at[:, pl.ds(pl.multiple_of(zb * 256, 256), 256)],
            basis_v.at[zb],
            basis_sem.at[zb],
        )

    def pp_load(h):
        return pltpu.make_async_copy(
            pp_hbm.at[:, pl.ds(h * 256, 256)], pp_v.at[h], pp_sem.at[h]
        )

    pp_load(0).start()
    for zb in range(4):
        basis_load(zb).start()
    pp_load(1).start()

    own_n = y_hi == cc
    own_c = jnp.logical_and(y == 2 * zl + cc, y_hi == cc)
    barrier = pltpu.get_barrier_semaphore()

    def greet(device):
        pl.semaphore_signal(barrier, inc=1, device_id=device, device_id_type=MESH)

    for d in range(1, 4):
        greet(dev(y=(y + 4 - d) % 4))
        greet(dev(zh=(zh + 4 - d) % 4))
    greet(dev(cc=1 - cc))
    for j in range(2):
        for pc in range(2):
            mine = jnp.logical_and(own_n, jnp.logical_and(y_lo == j, cc == pc))

            @pl.when(jnp.logical_not(mine))
            def _():
                greet(dev(y=2 * cc + j, cc=pc))

    for slot in range(8):
        source = dev(
            x=(x + 4 - slot // 2) % 4, zl=(zl + slot % 2) % 2, y=2 * zl + cc, cc=y_hi
        )
        if slot == 0:

            @pl.when(jnp.logical_not(own_c))
            def _():
                greet(source)
        else:
            greet(source)
    expected = 19 - jnp.where(own_n, 1, 0) - jnp.where(own_c, 1, 0)

    def y_copy(c, d):
        return pltpu.make_async_remote_copy(
            src_ref=psend.at[c, (y + d) % 4],
            dst_ref=yrecv.at[c, d - 1],
            send_sem=y_ss.at[c, d - 1],
            recv_sem=y_rs.at[c, d - 1],
            device_id=dev(y=(y + d) % 4),
            device_id_type=MESH,
        )

    def z_copy(c, d):
        return pltpu.make_async_remote_copy(
            src_ref=zsend.at[c, (zh + d) % 4],
            dst_ref=zrecv.at[c, d - 1],
            send_sem=z_ss.at[c, d - 1],
            recv_sem=z_rs.at[c, d - 1],
            device_id=dev(zh=(zh + d) % 4),
            device_id_type=MESH,
        )

    def m_copy(c, d):
        return pltpu.make_async_remote_copy(
            src_ref=mbuf.at[c, cc, zh],
            dst_ref=mbuf.at[c, cc, zh],
            send_sem=m_ss.at[c, d - 1],
            recv_sem=m_rs.at[c, d - 1],
            device_id=dev(zh=(zh + d) % 4),
            device_id_type=MESH,
        )

    def n_copy(c, d):
        return pltpu.make_async_remote_copy(
            src_ref=mbuf.at[c, cc, zh],
            dst_ref=nbuf.at[c, y_lo, cc],
            send_sem=n_ss.at[c, d],
            recv_sem=n_rs.at[c, y_lo * 2 + cc],
            device_id=dev(y=(y + d) % 4, cc=y_hi),
            device_id_type=MESH,
        )

    def n_arrival(c, j, pc):
        return pltpu.make_async_remote_copy(
            src_ref=mbuf.at[c, cc, zh],
            dst_ref=nbuf.at[c, j, pc],
            send_sem=n_ss.at[c, 0],
            recv_sem=n_rs.at[c, j * 2 + pc],
            device_id=dev(cc=1 - cc),
            device_id_type=MESH,
        )

    def relay(c):
        return pltpu.make_async_remote_copy(
            src_ref=mbuf.at[c, cc],
            dst_ref=mbuf.at[c, cc],
            send_sem=r_ss.at[c],
            recv_sem=r_rs.at[c],
            device_id=dev(cc=1 - cc),
            device_id_type=MESH,
        )

    w_copy = pltpu.make_async_remote_copy(
        src_ref=wbuf.at[cc],
        dst_ref=wbuf.at[cc],
        send_sem=w_ss,
        recv_sem=w_rs,
        device_id=dev(cc=1 - cc),
        device_id_type=MESH,
    )

    def c_copy(j, block):
        slot = ((block + 4 - x) % 4) * 2 + (y_hi + zl) % 2
        return pltpu.make_async_remote_copy(
            src_ref=csend.at[j, block],
            dst_ref=crecv.at[slot],
            send_sem=c_ss.at[j, block],
            recv_sem=c_rs.at[slot],
            device_id=dev(y=2 * cc + j, x=block, zl=y_hi, cc=y_lo),
            device_id_type=MESH,
        )

    def c_arrival(slot):
        return pltpu.make_async_remote_copy(
            src_ref=csend.at[0, 0],
            dst_ref=crecv.at[slot],
            send_sem=c_ss.at[0, 0],
            recv_sem=c_rs.at[slot],
            device_id=dev(cc=1 - cc),
            device_id_type=MESH,
        )

    def project(h):
        pp_load(h).wait()

        def rows(zb, carry):
            if h == 0:
                basis_load(zb).wait()
            block = lax.dot_general(
                basis_v[zb],
                pp_v[h],
                (((0,), (0,)), ((), ())),
                preferred_element_type=F32,
            )
            block = block.astype(BF16).reshape(4, 64, 256)
            psend[2 * h, :, zb] = block[:, :, :128]
            psend[2 * h + 1, :, zb] = block[:, :, 128:]
            return carry

        lax.fori_loop(0, 4, rows, 0)

    def send_y(c):
        for d in (2, 1, 3):
            y_copy(c, d).start()

    def make_weights():
        levels = lax.broadcasted_iota(jnp.int32, (128, 512), 0)

        def lookup(index, table):
            column = jnp.transpose(jnp.broadcast_to(table, (128, 128)))[:, :1]
            return jnp.sum(jnp.where(levels == index, column, 0.0), axis=0, keepdims=True)

        gap = lookup(cidx_ref[...], cond_ref[...]) - lookup(vidx_ref[...], val_ref[...])
        for k in range(8):
            freq = freq_ref[k]
            weight = -4.0 * gap / (gap * gap + freq * freq) / pairs_total
            for c in range(CHUNKS):
                wbuf[cc, c, k : k + 1, :] = weight[:, c * 128 : (c + 1) * 128]

    def stage_y(c):
        for d in range(1, 4):
            y_copy(c, d).wait_recv()
        total = psend[c, y].astype(F32)
        for d in range(3):
            total += yrecv[c, d].astype(F32)
        zsend[c] = total.astype(BF16)
        for d in (2, 1, 3):
            z_copy(c, d).start()

    def stage_z(c):
        for d in range(1, 4):
            z_copy(c, d).wait_recv()
        total = zsend[c, zh].astype(F32)
        for d in range(3):
            total += zrecv[c, d].astype(F32)
        own = total.astype(BF16)
        mbuf[c, cc, zh] = own

        @pl.when(own_n)
        def _():
            nbuf[c, y_lo, cc] = own

        for d in (2, 1, 3):
            m_copy(c, d).start()
        for d in (2, 1, 3):
            n_copy(c, d).start()

        @pl.when(jnp.logical_not(own_n))
        def _():
            n_copy(c, 0).start()

    def stage_relay(c):
        for d in range(1, 4):
            m_copy(c, d).wait_recv()
        relay(c).start()

    def stage_response(c):
        if c == 0:
            w_copy.wait_recv()
        for j in range(2):
            for pc in range(2):
                mine = jnp.logical_and(own_n, jnp.logical_and(y_lo == j, cc == pc))

                @pl.when(jnp.logical_not(mine))
                def _():
                    n_arrival(c, j, pc).wait_recv()

        relay(c).wait_recv()
        right = jnp.concatenate([mbuf[c, pc].reshape(256, 128) for pc in range(2)], axis=1)
        for j in range(2):
            left = jnp.concatenate(
                [
                    (wbuf[pc, c][:, None, :] * nbuf[c, j, pc].astype(F32)[None])
                    .astype(BF16)
                    .reshape(512, 128)
                    for pc in range(2)
                ],
                axis=1,
            )
            part = lax.dot_general(
                left, right, (((1,), (1,)), ((), ())), preferred_element_type=F32
            )
            if c == 0:
                acc[j] = part
            else:
                acc[j] += part

    def send_tiles(j):
        rows = acc[j].reshape(8, 64, 256)
        for block in range(4):
            lanes = rows[:, :, block * 64 : (block + 1) * 64]
            tile = jnp.concatenate([lanes[:, :32], lanes[:, 32:]], axis=2).astype(BF16)
            csend[j, block] = tile
            mine = jnp.logical_and(own_c, jnp.logical_and(y_lo == j, x == block))

            @pl.when(mine)
            def _():
                crecv[0] = tile

            @pl.when(jnp.logical_not(mine))
            def _():
                c_copy(j, block).start()

    project(0)
    pl.semaphore_wait(barrier, expected)
    send_y(0)
    send_y(1)
    project(1)
    send_y(2)
    send_y(3)
    make_weights()
    w_copy.start()
    for t in range(CHUNKS + 3):
        if t < CHUNKS:
            stage_y(t)
        if 0 <= t - 1 < CHUNKS:
            stage_z(t - 1)
        if 0 <= t - 2 < CHUNKS:
            stage_relay(t - 2)
        if 0 <= t - 3 < CHUNKS:
            stage_response(t - 3)
    for j in range(2):
        send_tiles(j)

    for c in range(CHUNKS):
        for d in range(1, 4):
            y_copy(c, d).wait_send()
            z_copy(c, d).wait_send()
            m_copy(c, d).wait_send()
            n_copy(c, d).wait_send()

        @pl.when(jnp.logical_not(own_n))
        def _():
            n_copy(c, 0).wait_send()

        relay(c).wait_send()
    w_copy.wait_send()

    @pl.when(jnp.logical_not(own_c))
    def _():
        c_arrival(0).wait_recv()

    total = crecv[0].astype(F32)
    for slot in range(1, 8):
        c_arrival(slot).wait_recv()
        total += crecv[slot].astype(F32)
    out_ref[:, :32, :] = total[:, :, :64]
    out_ref[:, 32:, :] = total[:, :, 64:]
    for j in range(2):
        for block in range(4):
            mine = jnp.logical_and(own_c, jnp.logical_and(y_lo == j, x == block))

            @pl.when(jnp.logical_not(mine))
            def _():
                c_copy(j, block).wait_send()


def per_device(
    pair_products, basis, val_energy, cond_energy, frequencies, valence_index, conduction_index
):
    pairs_total = pair_products.shape[1] * lax.axis_size("pair")
    vmem = pl.BlockSpec(memory_space=pltpu.VMEM)
    smem = pl.BlockSpec(memory_space=pltpu.SMEM)
    hbm = pl.BlockSpec(memory_space=pl.ANY)
    dma = pltpu.SemaphoreType.DMA
    return pl.pallas_call(
        functools.partial(kernel, pairs_total),
        out_shape=jax.ShapeDtypeStruct((8, 64, 64), F32),
        in_specs=[hbm, hbm, vmem, vmem, smem, vmem, vmem],
        out_specs=vmem,
        scratch_shapes=[
            pltpu.VMEM((4, 2048, 256), BF16),
            pltpu.VMEM((HALVES, 2048, 256), BF16),
            pltpu.VMEM((CHUNKS, 4, 4, 64, 128), BF16),
            pltpu.VMEM((CHUNKS, 3, 4, 64, 128), BF16),
            pltpu.VMEM((CHUNKS, 4, 64, 128), BF16),
            pltpu.VMEM((CHUNKS, 3, 64, 128), BF16),
            pltpu.VMEM((CHUNKS, 2, 4, 64, 128), BF16),
            pltpu.VMEM((CHUNKS, 2, 2, 64, 128), BF16),
            pltpu.VMEM((2, CHUNKS, 8, 128), F32),
            pltpu.VMEM((2, 512, 256), F32),
            pltpu.VMEM((2, 4, 8, 32, 128), BF16),
            pltpu.VMEM((8, 8, 32, 128), BF16),
            dma((4,)),
            dma((HALVES,)),
            dma((CHUNKS, 3)),
            dma((CHUNKS, 3)),
            dma((CHUNKS, 3)),
            dma((CHUNKS, 3)),
            dma((CHUNKS, 3)),
            dma((CHUNKS, 3)),
            dma((CHUNKS, 4)),
            dma((CHUNKS, 4)),
            dma((CHUNKS,)),
            dma((CHUNKS,)),
            dma(()),
            dma(()),
            dma((2, 4)),
            dma((8,)),
        ],
        compiler_params=pltpu.CompilerParams(
            collective_id=0, has_side_effects=True, vmem_limit_bytes=48 * 2**20
        ),
    )(
        pair_products,
        basis,
        val_energy.reshape(1, -1),
        cond_energy.reshape(1, -1),
        frequencies,
        valence_index.reshape(1, -1),
        conduction_index.reshape(1, -1),
    )


def solution(mesh):
    placed = (P("pw", "pair"), P("pw", None), P(), P(), P(), P("pair"), P("pair"))
    return jax.shard_map(
        per_device, mesh=mesh, in_specs=placed, out_specs=P(None, "pw", "pair"), check_vma=False
    )
```

time: 170 us -> 62.3 us (0.37)
  the two profiles are of different devices: /device:TPU:1 before, /device:TPU:30 now
where the time goes in v1:
time: 62.3 us; the launch traced here: 62.1 us
  Pallas kernels  56.5 us (91%)
  local copies, waits for them, and re-layouts  5.62 us (9%)
    pallas_call x1, Pallas kernels, per_device(): pl.pallas_call(functools.partial(kernel, pairs_total), out_shape=jax.Shap...  56.5 us
    unnamed x13, local copies, waits for them, and re-layouts  5.62 us

profile of v1, /device:TPU:30, one launch (start us, length us, event | category | flops | bytes accessed | tf_op | source)
XLA Modules:
  0.0 62.1 jit_solution(4863437036130110746)
XLA Ops:
  0.0 0.0 copy-start
  0.0 1.6 %copy-done = bf16[2048,512]{1,0:T(8,128)(2,1)S(1)} copy-done((bf16[2048,512]{1,0:T(8,128)(2,1)S(1)}, bf16[2048,512]{1,0:T(8,128)(2,1)}, u32[]{:S(2)}) %copy-start) | copy-done | bytes 2097176
  1.6 0.0 copy-start.1
  1.6 0.7 %copy-done.1 = s32[512]{0:T(512)S(1)} copy-done((s32[512]{0:T(512)S(1)}, s32[512]{0:T(512)}, u32[]{:S(2)}) %copy-start.1) | copy-done | bytes 2072
  2.3 0.0 copy-start.2
  2.3 0.7 %copy-done.2 = s32[512]{0:T(512)S(1)} copy-done((s32[512]{0:T(512)S(1)}, s32[512]{0:T(512)}, u32[]{:S(2)}) %copy-start.2) | copy-done | bytes 2072
  3.0 0.0 copy-start.3
  3.0 0.7 %copy-done.3 = f32[128]{0:T(128)S(1)} copy-done((f32[128]{0:T(128)S(1)}, f32[128]{0:T(128)}, u32[]{:S(2)}) %copy-start.3) | copy-done | bytes 536
  3.6 0.0 copy-start.4
  3.6 0.7 %copy-done.4 = f32[128]{0:T(128)S(1)} copy-done((f32[128]{0:T(128)S(1)}, f32[128]{0:T(128)}, u32[]{:S(2)}) %copy-start.4) | copy-done | bytes 536
  4.3 0.0 copy-start.5
  4.3 0.7 %copy-done.5 = f32[8]{0:T(128)S(1)} copy-done((f32[8]{0:T(128)S(1)}, f32[8]{0:T(128)}, u32[]{:S(2)}) %copy-start.5) | copy-done | bytes 56
  4.9 56.5 %shard_map.73 = f32[8,64,64]{2,1,0:T(8,128)S(1)} custom-call(bf16[2048,512]{1,0:T(8,128)(2,1)S(1)} %copy-done, bf16[2048,1024]{1,0:T(8,128)(2,1)} %basis_hbm.1, f32[1,128]{1,0:T(1,128)S(1)} %bitcast.6, f32[1,128]{1,0:T(1,128)S(1)} %bitcast.7, f32[8]{0:T(128)S(1)} %copy-done.5, s32[1,512]{1,0:T(1,128)S(1)} %bitcast.4, s32[1,512]{1,0:T(1,128)S(1)} %bitcast.5), custom_call_target="tpu_custom_call" | custom-call | tf_op jit(solution)/shard_map/pallas_call | solution.py:386
  61.4 0.7 %copy.9 = f32[8,64,64]{2,1,0:T(8,128)} copy(f32[8,64,64]{2,1,0:T(8,128)S(1)} %shard_map.73) | data formatting | bytes 262144
Async XLA Ops:
  0.0 1.6 %copy-start = (bf16[2048,512]{1,0:T(8,128)(2,1)S(1)}, bf16[2048,512]{1,0:T(8,128)(2,1)}, u32[]{:S(2)}) copy-start(bf16[2048,512]{1,0:T(8,128)(2,1)} %pp_hbm.1) | copy-start | bytes 6291460
  1.6 0.7 %copy-start.1 = (s32[512]{0:T(512)S(1)}, s32[512]{0:T(512)}, u32[]{:S(2)}) copy-start(s32[512]{0:T(512)} %param.12) | copy-start | bytes 6148
  2.3 0.7 %copy-start.2 = (s32[512]{0:T(512)S(1)}, s32[512]{0:T(512)}, u32[]{:S(2)}) copy-start(s32[512]{0:T(512)} %param.13) | copy-start | bytes 6148
  3.0 0.7 %copy-start.3 = (f32[128]{0:T(128)S(1)}, f32[128]{0:T(128)}, u32[]{:S(2)}) copy-start(f32[128]{0:T(128)} %param.9) | copy-start | bytes 1540
  3.6 0.7 %copy-start.4 = (f32[128]{0:T(128)S(1)}, f32[128]{0:T(128)}, u32[]{:S(2)}) copy-start(f32[128]{0:T(128)} %param.10) | copy-start | bytes 1540
  4.3 0.7 %copy-start.5 = (f32[8]{0:T(128)S(1)}, f32[8]{0:T(128)}, u32[]{:S(2)}) copy-start(f32[8]{0:T(128)} %freq_ref.1) | copy-start | bytes 100

commit v2 on v1

--- a/solution.py
+++ b/solution.py
@@ -18,12 +18,18 @@
     pairs_total,
     pp_hbm,
     basis_hbm,
+    val_hbm,
+    cond_hbm,
+    freq_hbm,
+    vidx_hbm,
+    cidx_hbm,
+    out_ref,
     val_ref,
     cond_ref,
     freq_ref,
     vidx_ref,
     cidx_ref,
-    out_ref,
+    small_sem,
     basis_v,
     pp_v,
     psend,
@@ -35,7 +41,9 @@
     wbuf,
     acc,
     csend,
-    crecv,
+    xrecv,
+    fsend,
+    frecv,
     basis_sem,
     pp_sem,
     y_ss,
@@ -50,8 +58,10 @@
     r_rs,
     w_ss,
     w_rs,
-    c_ss,
-    c_rs,
+    x_ss,
+    x_rs,
+    f_ss,
+    f_rs,
 ):
     pair, pw = lax.axis_index("pair"), lax.axis_index("pw")
     x, zl, cc = pair // 4, (pair // 2) % 2, pair % 2
@@ -77,6 +87,20 @@
     for zb in range(4):
         basis_load(zb).start()
     pp_load(1).start()
+    small_loads = [
+        pltpu.make_async_copy(source, target, small_sem.at[i])
+        for i, (source, target) in enumerate(
+            [
+                (val_hbm, val_ref),
+                (cond_hbm, cond_ref),
+                (freq_hbm, freq_ref),
+                (vidx_hbm, vidx_ref),
+                (cidx_hbm, cidx_ref),
+            ]
+        )
+    ]
+    for load in small_loads:
+        load.start()
 
     own_n = y_hi == cc
     own_c = jnp.logical_and(y == 2 * zl + cc, y_hi == cc)
@@ -88,6 +112,7 @@
     for d in range(1, 4):
         greet(dev(y=(y + 4 - d) % 4))
         greet(dev(zh=(zh + 4 - d) % 4))
+        greet(dev(x=(x + 4 - d) % 4))
     greet(dev(cc=1 - cc))
     for j in range(2):
         for pc in range(2):
@@ -97,18 +122,13 @@
             def _():
                 greet(dev(y=2 * cc + j, cc=pc))
 
-    for slot in range(8):
-        source = dev(
-            x=(x + 4 - slot // 2) % 4, zl=(zl + slot % 2) % 2, y=2 * zl + cc, cc=y_hi
-        )
-        if slot == 0:
-
-            @pl.when(jnp.logical_not(own_c))
-            def _():
-                greet(source)
-        else:
-            greet(source)
-    expected = 19 - jnp.where(own_n, 1, 0) - jnp.where(own_c, 1, 0)
+    greet(dev(zl=1 - zl, y=2 * zl + cc, cc=y_hi))
+
+    @pl.when(jnp.logical_not(own_c))
+    def _():
+        greet(dev(y=2 * zl + cc, cc=y_hi))
+
+    expected = 16 - jnp.where(own_n, 1, 0) - jnp.where(own_c, 1, 0)
 
     def y_copy(c, d):
         return pltpu.make_async_remote_copy(
@@ -179,23 +199,33 @@
         device_id_type=MESH,
     )
 
-    def c_copy(j, block):
-        slot = ((block + 4 - x) % 4) * 2 + (y_hi + zl) % 2
-        return pltpu.make_async_remote_copy(
-            src_ref=csend.at[j, block],
-            dst_ref=crecv.at[slot],
-            send_sem=c_ss.at[j, block],
-            recv_sem=c_rs.at[slot],
-            device_id=dev(y=2 * cc + j, x=block, zl=y_hi, cc=y_lo),
-            device_id_type=MESH,
-        )
-
-    def c_arrival(slot):
-        return pltpu.make_async_remote_copy(
-            src_ref=csend.at[0, 0],
-            dst_ref=crecv.at[slot],
-            send_sem=c_ss.at[0, 0],
-            recv_sem=c_rs.at[slot],
+    def x_copy(j, d):
+        return pltpu.make_async_remote_copy(
+            src_ref=csend.at[j, (x + d) % 4],
+            dst_ref=xrecv.at[j, d - 1],
+            send_sem=x_ss.at[j, d - 1],
+            recv_sem=x_rs.at[j, d - 1],
+            device_id=dev(x=(x + d) % 4),
+            device_id_type=MESH,
+        )
+
+    def f_copy(j):
+        slot = (y_hi + zl) % 2
+        return pltpu.make_async_remote_copy(
+            src_ref=fsend.at[j],
+            dst_ref=frecv.at[slot],
+            send_sem=f_ss.at[j],
+            recv_sem=f_rs.at[slot],
+            device_id=dev(y=2 * cc + j, zl=y_hi, cc=y_lo),
+            device_id_type=MESH,
+        )
+
+    def f_arrival(slot):
+        return pltpu.make_async_remote_copy(
+            src_ref=fsend.at[0],
+            dst_ref=frecv.at[slot],
+            send_sem=f_ss.at[0],
+            recv_sem=f_rs.at[slot],
             device_id=dev(cc=1 - cc),
             device_id_type=MESH,
         )
@@ -224,6 +254,8 @@
             y_copy(c, d).start()
 
     def make_weights():
+        for load in small_loads:
+            load.wait()
         levels = lax.broadcasted_iota(jnp.int32, (128, 512), 0)
 
         def lookup(index, table):
@@ -311,15 +343,26 @@
             lanes = rows[:, :, block * 64 : (block + 1) * 64]
             tile = jnp.concatenate([lanes[:, :32], lanes[:, 32:]], axis=2).astype(BF16)
             csend[j, block] = tile
-            mine = jnp.logical_and(own_c, jnp.logical_and(y_lo == j, x == block))
-
-            @pl.when(mine)
-            def _():
-                crecv[0] = tile
-
-            @pl.when(jnp.logical_not(mine))
-            def _():
-                c_copy(j, block).start()
+        for d in (2, 1, 3):
+            x_copy(j, d).start()
+
+    def stage_x(j):
+        for d in range(1, 4):
+            x_copy(j, d).wait_recv()
+        total = csend[j, x].astype(F32)
+        for d in range(3):
+            total += xrecv[j, d].astype(F32)
+        tile = total.astype(BF16)
+        fsend[j] = tile
+        mine = jnp.logical_and(own_c, y_lo == j)
+
+        @pl.when(mine)
+        def _():
+            frecv[0] = tile
+
+        @pl.when(jnp.logical_not(mine))
+        def _():
+            f_copy(j).start()
 
     project(0)
     pl.semaphore_wait(barrier, expected)
@@ -341,6 +384,8 @@
             stage_response(t - 3)
     for j in range(2):
         send_tiles(j)
+    for j in range(2):
+        stage_x(j)
 
     for c in range(CHUNKS):
         for d in range(1, 4):
@@ -355,24 +400,24 @@
 
         relay(c).wait_send()
     w_copy.wait_send()
+    for j in range(2):
+        for d in range(1, 4):
+            x_copy(j, d).wait_send()
 
     @pl.when(jnp.logical_not(own_c))
     def _():
-        c_arrival(0).wait_recv()
-
-    total = crecv[0].astype(F32)
-    for slot in range(1, 8):
-        c_arrival(slot).wait_recv()
-        total += crecv[slot].astype(F32)
+        f_arrival(0).wait_recv()
+
+    f_arrival(1).wait_recv()
+    total = frecv[0].astype(F32) + frecv[1].astype(F32)
     out_ref[:, :32, :] = total[:, :, :64]
     out_ref[:, 32:, :] = total[:, :, 64:]
     for j in range(2):
-        for block in range(4):
-            mine = jnp.logical_and(own_c, jnp.logical_and(y_lo == j, x == block))
-
-            @pl.when(jnp.logical_not(mine))
-            def _():
-                c_copy(j, block).wait_send()
+        mine = jnp.logical_and(own_c, y_lo == j)
+
+        @pl.when(jnp.logical_not(mine))
+        def _():
+            f_copy(j).wait_send()
 
 
 def per_device(
@@ -380,15 +425,20 @@
 ):
     pairs_total = pair_products.shape[1] * lax.axis_size("pair")
     vmem = pl.BlockSpec(memory_space=pltpu.VMEM)
-    smem = pl.BlockSpec(memory_space=pltpu.SMEM)
     hbm = pl.BlockSpec(memory_space=pl.ANY)
     dma = pltpu.SemaphoreType.DMA
     return pl.pallas_call(
         functools.partial(kernel, pairs_total),
         out_shape=jax.ShapeDtypeStruct((8, 64, 64), F32),
-        in_specs=[hbm, hbm, vmem, vmem, smem, vmem, vmem],
+        in_specs=[hbm] * 7,
         out_specs=vmem,
         scratch_shapes=[
+            pltpu.VMEM((1, 128), F32),
+            pltpu.VMEM((1, 128), F32),
+            pltpu.SMEM((8,), F32),
+            pltpu.VMEM((1, 512), jnp.int32),
+            pltpu.VMEM((1, 512), jnp.int32),
+            dma((5,)),
             pltpu.VMEM((4, 2048, 256), BF16),
             pltpu.VMEM((HALVES, 2048, 256), BF16),
             pltpu.VMEM((CHUNKS, 4, 4, 64, 128), BF16),
@@ -400,7 +450,9 @@
             pltpu.VMEM((2, CHUNKS, 8, 128), F32),
             pltpu.VMEM((2, 512, 256), F32),
             pltpu.VMEM((2, 4, 8, 32, 128), BF16),
-            pltpu.VMEM((8, 8, 32, 128), BF16),
+            pltpu.VMEM((2, 3, 8, 32, 128), BF16),
+            pltpu.VMEM((2, 8, 32, 128), BF16),
+            pltpu.VMEM((2, 8, 32, 128), BF16),
             dma((4,)),
             dma((HALVES,)),
             dma((CHUNKS, 3)),
@@ -415,11 +467,13 @@
             dma((CHUNKS,)),
             dma(()),
             dma(()),
-            dma((2, 4)),
-            dma((8,)),
+            dma((2, 3)),
+            dma((2, 3)),
+            dma((2,)),
+            dma((2,)),
         ],
         compiler_params=pltpu.CompilerParams(
-            collective_id=0, has_side_effects=True, vmem_limit_bytes=48 * 2**20
+            collective_id=0, has_side_effects=True, vmem_limit_bytes=60 * 2**20
         ),
     )(
         pair_products,

time: 62.3 us -> 52.4 us (0.84)
  the two profiles are of different devices: /device:TPU:30 before, /device:TPU:1 now
where the time goes in v2:
time: 52.4 us; the launch traced here: 52.3 us
  Pallas kernels  50.6 us (97%)
  local copies, waits for them, and re-layouts  1.67 us (3%)
    pallas_call x1, Pallas kernels, per_device(): pl.pallas_call(functools.partial(kernel, pairs_total), out_shape=jax.Shap...  50.6 us
    unnamed x1, local copies, waits for them, and re-layouts  1.67 us

profile of v2, /device:TPU:1, one launch (start us, length us, event | category | flops | bytes accessed | tf_op | source)
XLA Modules:
  0.0 52.3 jit_solution(10233386417013077524)
XLA Ops:
  0.0 50.6 %shard_map.73 = f32[8,64,64]{2,1,0:T(8,128)} custom-call(bf16[2048,512]{1,0:T(8,128)(2,1)} %pp_hbm.1, bf16[2048,1024]{1,0:T(8,128)(2,1)} %basis_hbm.1, f32[1,128]{1,0:T(1,128)} %bitcast.6, f32[1,128]{1,0:T(1,128)} %bitcast.7, f32[8]{0:T(128)} %freq_hbm.1, s32[1,512]{1,0:T(1,128)} %bitcast.4, s32[1,512]{1,0:T(1,128)} %bitcast.5), custom_call_target="tpu_custom_call" | custom-call | tf_op jit(solution)/shard_map/pallas_call | solution.py:430
  50.7 1.7 %copy.9 = f32[8,64,64]{2,1,0:T(8,128)} copy(f32[8,64,64]{2,1,0:T(8,128)} %shard_map.73) | data formatting | bytes 262144

commit v3 on v2

--- a/solution.py
+++ b/solution.py
@@ -36,12 +36,11 @@
     yrecv,
     zsend,
     zrecv,
+    own_rows,
     mbuf,
     nbuf,
     wbuf,
     acc,
-    csend,
-    xrecv,
     fsend,
     frecv,
     basis_sem,
@@ -54,12 +53,14 @@
     m_rs,
     n_ss,
     n_rs,
+    nx_ss,
+    nx_rs,
     r_ss,
     r_rs,
     w_ss,
     w_rs,
-    x_ss,
-    x_rs,
+    wx_ss,
+    wx_rs,
     f_ss,
     f_rs,
 ):
@@ -103,6 +104,7 @@
         load.start()
 
     own_n = y_hi == cc
+    own_m = x == zh
     own_c = jnp.logical_and(y == 2 * zl + cc, y_hi == cc)
     barrier = pltpu.get_barrier_semaphore()
 
@@ -114,6 +116,15 @@
         greet(dev(zh=(zh + 4 - d) % 4))
         greet(dev(x=(x + 4 - d) % 4))
     greet(dev(cc=1 - cc))
+    for e in range(4):
+        source = dev(x=(x + e) % 4, zh=x)
+        if e == 0:
+
+            @pl.when(jnp.logical_not(own_m))
+            def _():
+                greet(source)
+        else:
+            greet(source)
     for j in range(2):
         for pc in range(2):
             mine = jnp.logical_and(own_n, jnp.logical_and(y_lo == j, cc == pc))
@@ -128,7 +139,7 @@
     def _():
         greet(dev(y=2 * zl + cc, cc=y_hi))
 
-    expected = 16 - jnp.where(own_n, 1, 0) - jnp.where(own_c, 1, 0)
+    expected = 20 - jnp.where(own_m, 1, 0) - jnp.where(own_n, 1, 0) - jnp.where(own_c, 1, 0)
 
     def y_copy(c, d):
         return pltpu.make_async_remote_copy(
@@ -140,6 +151,16 @@
             device_id_type=MESH,
         )
 
+    def y_part(c, d, zb):
+        return pltpu.make_async_remote_copy(
+            src_ref=psend.at[c, (y + d) % 4, zb],
+            dst_ref=yrecv.at[c, d - 1, zb],
+            send_sem=y_ss.at[c, d - 1],
+            recv_sem=y_rs.at[c, d - 1],
+            device_id=dev(y=(y + d) % 4),
+            device_id_type=MESH,
+        )
+
     def z_copy(c, d):
         return pltpu.make_async_remote_copy(
             src_ref=zsend.at[c, (zh + d) % 4],
@@ -152,18 +173,28 @@
 
     def m_copy(c, d):
         return pltpu.make_async_remote_copy(
-            src_ref=mbuf.at[c, cc, zh],
-            dst_ref=mbuf.at[c, cc, zh],
-            send_sem=m_ss.at[c, d - 1],
-            recv_sem=m_rs.at[c, d - 1],
-            device_id=dev(zh=(zh + d) % 4),
+            src_ref=own_rows.at[c],
+            dst_ref=mbuf.at[c, cc, x],
+            send_sem=m_ss.at[c, d],
+            recv_sem=m_rs.at[c, x],
+            device_id=dev(x=zh, zh=(zh + d) % 4),
+            device_id_type=MESH,
+        )
+
+    def m_arrival(c, e):
+        return pltpu.make_async_remote_copy(
+            src_ref=own_rows.at[c],
+            dst_ref=mbuf.at[c, cc, (x + e) % 4],
+            send_sem=m_ss.at[c, 0],
+            recv_sem=m_rs.at[c, (x + e) % 4],
+            device_id=dev(cc=1 - cc),
             device_id_type=MESH,
         )
 
     def n_copy(c, d):
         return pltpu.make_async_remote_copy(
-            src_ref=mbuf.at[c, cc, zh],
-            dst_ref=nbuf.at[c, y_lo, cc],
+            src_ref=own_rows.at[c],
+            dst_ref=nbuf.at[c, x, y_lo, cc],
             send_sem=n_ss.at[c, d],
             recv_sem=n_rs.at[c, y_lo * 2 + cc],
             device_id=dev(y=(y + d) % 4, cc=y_hi),
@@ -172,11 +203,21 @@
 
     def n_arrival(c, j, pc):
         return pltpu.make_async_remote_copy(
-            src_ref=mbuf.at[c, cc, zh],
-            dst_ref=nbuf.at[c, j, pc],
+            src_ref=own_rows.at[c],
+            dst_ref=nbuf.at[c, x, j, pc],
             send_sem=n_ss.at[c, 0],
             recv_sem=n_rs.at[c, j * 2 + pc],
             device_id=dev(cc=1 - cc),
+            device_id_type=MESH,
+        )
+
+    def nx_copy(c, d):
+        return pltpu.make_async_remote_copy(
+            src_ref=nbuf.at[c, x],
+            dst_ref=nbuf.at[c, x],
+            send_sem=nx_ss.at[c, d - 1],
+            recv_sem=nx_rs.at[c, d - 1],
+            device_id=dev(x=(x + d) % 4),
             device_id_type=MESH,
         )
 
@@ -190,25 +231,25 @@
             device_id_type=MESH,
         )
 
+    def wx_copy(d):
+        return pltpu.make_async_remote_copy(
+            src_ref=wbuf.at[x],
+            dst_ref=wbuf.at[x],
+            send_sem=wx_ss.at[d - 1],
+            recv_sem=wx_rs.at[d - 1],
+            device_id=dev(x=(x + d) % 4),
+            device_id_type=MESH,
+        )
+
     w_copy = pltpu.make_async_remote_copy(
-        src_ref=wbuf.at[cc],
-        dst_ref=wbuf.at[cc],
+        src_ref=wbuf.at[x, cc],
+        dst_ref=wbuf.at[x, cc],
         send_sem=w_ss,
         recv_sem=w_rs,
         device_id=dev(cc=1 - cc),
         device_id_type=MESH,
     )
 
-    def x_copy(j, d):
-        return pltpu.make_async_remote_copy(
-            src_ref=csend.at[j, (x + d) % 4],
-            dst_ref=xrecv.at[j, d - 1],
-            send_sem=x_ss.at[j, d - 1],
-            recv_sem=x_rs.at[j, d - 1],
-            device_id=dev(x=(x + d) % 4),
-            device_id_type=MESH,
-        )
-
     def f_copy(j):
         slot = (y_hi + zl) % 2
         return pltpu.make_async_remote_copy(
@@ -230,28 +271,21 @@
             device_id_type=MESH,
         )
 
-    def project(h):
-        pp_load(h).wait()
-
-        def rows(zb, carry):
-            if h == 0:
-                basis_load(zb).wait()
-            block = lax.dot_general(
-                basis_v[zb],
-                pp_v[h],
-                (((0,), (0,)), ((), ())),
-                preferred_element_type=F32,
-            )
-            block = block.astype(BF16).reshape(4, 64, 256)
-            psend[2 * h, :, zb] = block[:, :, :128]
-            psend[2 * h + 1, :, zb] = block[:, :, 128:]
-            return carry
-
-        lax.fori_loop(0, 4, rows, 0)
+    def project_rows(h, zb):
+        block = lax.dot_general(
+            basis_v[zb], pp_v[h], (((0,), (0,)), ((), ())), preferred_element_type=F32
+        )
+        block = block.astype(BF16).reshape(4, 64, 256)
+        psend[2 * h, :, zb] = block[:, :, :128]
+        psend[2 * h + 1, :, zb] = block[:, :, 128:]
 
     def send_y(c):
         for d in (2, 1, 3):
             y_copy(c, d).start()
+
+    def send_y_part(c, zb):
+        for d in (2, 1, 3):
+            y_part(c, d, zb).start()
 
     def make_weights():
         for load in small_loads:
@@ -267,7 +301,7 @@
             freq = freq_ref[k]
             weight = -4.0 * gap / (gap * gap + freq * freq) / pairs_total
             for c in range(CHUNKS):
-                wbuf[cc, c, k : k + 1, :] = weight[:, c * 128 : (c + 1) * 128]
+                wbuf[x, cc, c, k : k + 1, :] = weight[:, c * 128 : (c + 1) * 128]
 
     def stage_y(c):
         for d in range(1, 4):
@@ -286,29 +320,31 @@
         for d in range(3):
             total += zrecv[c, d].astype(F32)
         own = total.astype(BF16)
-        mbuf[c, cc, zh] = own
+        own_rows[c] = own
+
+        @pl.when(own_m)
+        def _():
+            mbuf[c, cc, x] = own
 
         @pl.when(own_n)
         def _():
-            nbuf[c, y_lo, cc] = own
+            nbuf[c, x, y_lo, cc] = own
+
+        for d in (2, 1, 3):
+            n_copy(c, d).start()
+
+        @pl.when(jnp.logical_not(own_n))
+        def _():
+            n_copy(c, 0).start()
 
         for d in (2, 1, 3):
             m_copy(c, d).start()
-        for d in (2, 1, 3):
-            n_copy(c, d).start()
-
-        @pl.when(jnp.logical_not(own_n))
-        def _():
-            n_copy(c, 0).start()
+
+        @pl.when(jnp.logical_not(own_m))
+        def _():
+            m_copy(c, 0).start()
 
     def stage_relay(c):
-        for d in range(1, 4):
-            m_copy(c, d).wait_recv()
-        relay(c).start()
-
-    def stage_response(c):
-        if c == 0:
-            w_copy.wait_recv()
         for j in range(2):
             for pc in range(2):
                 mine = jnp.logical_and(own_n, jnp.logical_and(y_lo == j, cc == pc))
@@ -317,42 +353,46 @@
                 def _():
                     n_arrival(c, j, pc).wait_recv()
 
+        for d in (2, 1, 3):
+            nx_copy(c, d).start()
+
+        @pl.when(jnp.logical_not(own_m))
+        def _():
+            m_arrival(c, 0).wait_recv()
+
+        for e in range(1, 4):
+            m_arrival(c, e).wait_recv()
+        relay(c).start()
+
+    def stage_response(c):
+        if c == 0:
+            for d in range(1, 4):
+                wx_copy(d).wait_recv()
         relay(c).wait_recv()
-        right = jnp.concatenate([mbuf[c, pc].reshape(256, 128) for pc in range(2)], axis=1)
-        for j in range(2):
-            left = jnp.concatenate(
-                [
-                    (wbuf[pc, c][:, None, :] * nbuf[c, j, pc].astype(F32)[None])
-                    .astype(BF16)
-                    .reshape(512, 128)
-                    for pc in range(2)
-                ],
-                axis=1,
-            )
-            part = lax.dot_general(
-                left, right, (((1,), (1,)), ((), ())), preferred_element_type=F32
-            )
-            if c == 0:
-                acc[j] = part
-            else:
-                acc[j] += part
-
-    def send_tiles(j):
-        rows = acc[j].reshape(8, 64, 256)
-        for block in range(4):
-            lanes = rows[:, :, block * 64 : (block + 1) * 64]
-            tile = jnp.concatenate([lanes[:, :32], lanes[:, 32:]], axis=2).astype(BF16)
-            csend[j, block] = tile
-        for d in (2, 1, 3):
-            x_copy(j, d).start()
-
-    def stage_x(j):
+        groups = [(xs, pc) for xs in range(4) for pc in range(2)]
+        left = jnp.concatenate(
+            [
+                (wbuf[xs, pc, c][:, None, :] * mbuf[c, pc, xs].astype(F32)[None])
+                .astype(BF16)
+                .reshape(512, 128)
+                for xs, pc in groups
+            ],
+            axis=1,
+        )
         for d in range(1, 4):
-            x_copy(j, d).wait_recv()
-        total = csend[j, x].astype(F32)
-        for d in range(3):
-            total += xrecv[j, d].astype(F32)
-        tile = total.astype(BF16)
+            nx_copy(c, d).wait_recv()
+        right = jnp.concatenate(
+            [nbuf[c, xs, :, pc].reshape(128, 128) for xs, pc in groups], axis=1
+        )
+        part = lax.dot_general(left, right, (((1,), (1,)), ((), ())), preferred_element_type=F32)
+        if c == 0:
+            acc[...] = part
+        else:
+            acc[...] += part
+
+    def send_tile(j):
+        rows = acc[...].reshape(8, 64, 128)[:, :, j * 64 : (j + 1) * 64]
+        tile = jnp.concatenate([rows[:, :32], rows[:, 32:]], axis=2).astype(BF16)
         fsend[j] = tile
         mine = jnp.logical_and(own_c, y_lo == j)
 
@@ -364,15 +404,34 @@
         def _():
             f_copy(j).start()
 
-    project(0)
+    pp_load(0).wait()
+    basis_load(0).wait()
+    project_rows(0, 0)
     pl.semaphore_wait(barrier, expected)
-    send_y(0)
+    send_y_part(0, 0)
+
+    def first_rows(zb, carry):
+        basis_load(zb).wait()
+        project_rows(0, zb)
+        send_y_part(0, zb)
+        return carry
+
+    lax.fori_loop(1, 4, first_rows, 0)
     send_y(1)
-    project(1)
+    pp_load(1).wait()
+
+    def second_rows(zb, carry):
+        project_rows(1, zb)
+        return carry
+
+    lax.fori_loop(0, 4, second_rows, 0)
     send_y(2)
     send_y(3)
     make_weights()
     w_copy.start()
+    w_copy.wait_recv()
+    for d in range(1, 4):
+        wx_copy(d).start()
     for t in range(CHUNKS + 3):
         if t < CHUNKS:
             stage_y(t)
@@ -383,9 +442,7 @@
         if 0 <= t - 3 < CHUNKS:
             stage_response(t - 3)
     for j in range(2):
-        send_tiles(j)
-    for j in range(2):
-        stage_x(j)
+        send_tile(j)
 
     for c in range(CHUNKS):
         for d in range(1, 4):
@@ -393,16 +450,20 @@
             z_copy(c, d).wait_send()
             m_copy(c, d).wait_send()
             n_copy(c, d).wait_send()
+            nx_copy(c, d).wait_send()
 
         @pl.when(jnp.logical_not(own_n))
         def _():
             n_copy(c, 0).wait_send()
+
+        @pl.when(jnp.logical_not(own_m))
+        def _():
+            m_copy(c, 0).wait_send()
 
         relay(c).wait_send()
     w_copy.wait_send()
-    for j in range(2):
-        for d in range(1, 4):
-            x_copy(j, d).wait_send()
+    for d in range(1, 4):
+        wx_copy(d).wait_send()
 
     @pl.when(jnp.logical_not(own_c))
     def _():
@@ -410,8 +471,8 @@
 
     f_arrival(1).wait_recv()
     total = frecv[0].astype(F32) + frecv[1].astype(F32)
-    out_ref[:, :32, :] = total[:, :, :64]
-    out_ref[:, 32:, :] = total[:, :, 64:]
+    rows = jnp.concatenate([total[:, :, :64], total[:, :, 64:]], axis=1)
+    out_ref[...] = jnp.swapaxes(rows, 1, 2)
     for j in range(2):
         mine = jnp.logical_and(own_c, y_lo == j)
 
@@ -445,12 +506,11 @@
             pltpu.VMEM((CHUNKS, 3, 4, 64, 128), BF16),
             pltpu.VMEM((CHUNKS, 4, 64, 128), BF16),
             pltpu.VMEM((CHUNKS, 3, 64, 128), BF16),
+            pltpu.VMEM((CHUNKS, 64, 128), BF16),
             pltpu.VMEM((CHUNKS, 2, 4, 64, 128), BF16),
-            pltpu.VMEM((CHUNKS, 2, 2, 64, 128), BF16),
-            pltpu.VMEM((2, CHUNKS, 8, 128), F32),
-            pltpu.VMEM((2, 512, 256), F32),
-            pltpu.VMEM((2, 4, 8, 32, 128), BF16),
-            pltpu.VMEM((2, 3, 8, 32, 128), BF16),
+            pltpu.VMEM((CHUNKS, 4, 2, 2, 64, 128), BF16),
+            pltpu.VMEM((4, 2, CHUNKS, 8, 128), F32),
+            pltpu.VMEM((512, 128), F32),
             pltpu.VMEM((2, 8, 32, 128), BF16),
             pltpu.VMEM((2, 8, 32, 128), BF16),
             dma((4,)),
@@ -459,21 +519,23 @@
             dma((CHUNKS, 3)),
             dma((CHUNKS, 3)),
             dma((CHUNKS, 3)),
+            dma((CHUNKS, 4)),
+            dma((CHUNKS, 4)),
+            dma((CHUNKS, 4)),
+            dma((CHUNKS, 4)),
             dma((CHUNKS, 3)),
             dma((CHUNKS, 3)),
-            dma((CHUNKS, 4)),
-            dma((CHUNKS, 4)),
             dma((CHUNKS,)),
             dma((CHUNKS,)),
             dma(()),
             dma(()),
-            dma((2, 3)),
-            dma((2, 3)),
+            dma((3,)),
+            dma((3,)),
             dma((2,)),
             dma((2,)),
         ],
         compiler_params=pltpu.CompilerParams(
-            collective_id=0, has_side_effects=True, vmem_limit_bytes=60 * 2**20
+            collective_id=0, has_side_effects=True, vmem_limit_bytes=56 * 2**20
         ),
     )(
         pair_products,

time: 52.4 us -> 50.5 us (0.964)
  Pallas kernels: 50.6 us -> 48.7 us
    pallas_call x1, Pallas kernels: 50.6 us -> 48.7 us  [per_device(): pl.pallas_call(functools.partial(kernel, pairs_total), out_shape=jax.Shap...]
where the time goes in v3:
time: 50.5 us; the launch traced here: 50.4 us
  Pallas kernels  48.7 us (96%)
  local copies, waits for them, and re-layouts  1.67 us (3%)
    pallas_call x1, Pallas kernels, per_device(): pl.pallas_call(functools.partial(kernel, pairs_total), out_shape=jax.Shap...  48.7 us
    unnamed x1, local copies, waits for them, and re-layouts  1.67 us

profile of v3, /device:TPU:1, one launch (start us, length us, event | category | flops | bytes accessed | tf_op | source)
XLA Modules:
  0.0 50.4 jit_solution(8518760975560418504)
XLA Ops:
  0.0 48.7 %shard_map.73 = f32[8,64,64]{2,1,0:T(8,128)} custom-call(bf16[2048,512]{1,0:T(8,128)(2,1)} %pp_hbm.1, bf16[2048,1024]{1,0:T(8,128)(2,1)} %basis_hbm.1, f32[1,128]{1,0:T(1,128)} %bitcast.6, f32[1,128]{1,0:T(1,128)} %bitcast.7, f32[8]{0:T(128)} %freq_hbm.1, s32[1,512]{1,0:T(1,128)} %bitcast.4, s32[1,512]{1,0:T(1,128)} %bitcast.5), custom_call_target="tpu_custom_call" | custom-call | tf_op jit(solution)/shard_map/pallas_call | solution.py:491
  48.7 1.7 %copy.9 = f32[8,64,64]{2,1,0:T(8,128)} copy(f32[8,64,64]{2,1,0:T(8,128)} %shard_map.73) | data formatting | bytes 262144

commit v4 on v3

--- a/solution.py
+++ b/solution.py
@@ -12,6 +12,7 @@
 MESH = pl.DeviceIdType.MESH
 CHUNKS = 4
 HALVES = 2
+LAST = CHUNKS - 1
 
 
 def kernel(
@@ -33,6 +34,8 @@
     basis_v,
     pp_v,
     psend,
+    passing,
+    passed_on,
     yrecv,
     zsend,
     zrecv,
@@ -53,6 +56,8 @@
     m_rs,
     n_ss,
     n_rs,
+    last_ss,
+    last_rs,
     nx_ss,
     nx_rs,
     r_ss,
@@ -128,10 +133,15 @@
     for j in range(2):
         for pc in range(2):
             mine = jnp.logical_and(own_n, jnp.logical_and(y_lo == j, cc == pc))
-
-            @pl.when(jnp.logical_not(mine))
-            def _():
-                greet(dev(y=2 * cc + j, cc=pc))
+            for e in range(4):
+                source = dev(x=(x + e) % 4, y=2 * cc + j, cc=pc)
+                if e == 0:
+
+                    @pl.when(jnp.logical_not(mine))
+                    def _():
+                        greet(source)
+                else:
+                    greet(source)
 
     greet(dev(zl=1 - zl, y=2 * zl + cc, cc=y_hi))
 
@@ -139,27 +149,33 @@
     def _():
         greet(dev(y=2 * zl + cc, cc=y_hi))
 
-    expected = 20 - jnp.where(own_m, 1, 0) - jnp.where(own_n, 1, 0) - jnp.where(own_c, 1, 0)
-
-    def y_copy(c, d):
-        return pltpu.make_async_remote_copy(
-            src_ref=psend.at[c, (y + d) % 4],
-            dst_ref=yrecv.at[c, d - 1],
-            send_sem=y_ss.at[c, d - 1],
-            recv_sem=y_rs.at[c, d - 1],
-            device_id=dev(y=(y + d) % 4),
-            device_id_type=MESH,
-        )
-
-    def y_part(c, d, zb):
-        return pltpu.make_async_remote_copy(
-            src_ref=psend.at[c, (y + d) % 4, zb],
-            dst_ref=yrecv.at[c, d - 1, zb],
-            send_sem=y_ss.at[c, d - 1],
-            recv_sem=y_rs.at[c, d - 1],
-            device_id=dev(y=(y + d) % 4),
-            device_id_type=MESH,
-        )
+    expected = 32 - jnp.where(own_m, 1, 0) - jnp.where(own_n, 1, 0) - jnp.where(own_c, 1, 0)
+
+    def to_y(source, target, c, i, step):
+        return pltpu.make_async_remote_copy(
+            src_ref=source,
+            dst_ref=target,
+            send_sem=y_ss.at[c, i],
+            recv_sem=y_rs.at[c, i],
+            device_id=dev(y=(y + step) % 4),
+            device_id_type=MESH,
+        )
+
+    def y_copies(c):
+        if c == LAST:
+            return [
+                functools.partial(to_y, psend.at[c, (y + d) % 4], yrecv.at[c, d - 1], c, d - 1, d)
+                for d in (2, 1, 3)
+            ]
+        low, high = pl.ds(0, 2), pl.ds(2, 2)
+        return [
+            functools.partial(to_y, psend.at[c, (y + 2) % 4, low], passing.at[c, 0], c, 0, 1),
+            functools.partial(to_y, psend.at[c, (y + 3) % 4, low], yrecv.at[c, 1, low], c, 3, 3),
+            functools.partial(to_y, psend.at[c, (y + 2) % 4, high], passing.at[c, 1], c, 1, 3),
+            functools.partial(to_y, psend.at[c, (y + 1) % 4, high], yrecv.at[c, 0, high], c, 2, 1),
+            functools.partial(to_y, passed_on.at[c, 0], yrecv.at[c, 0, low], c, 4, 1),
+            functools.partial(to_y, passed_on.at[c, 1], yrecv.at[c, 1, high], c, 5, 3),
+        ]
 
     def z_copy(c, d):
         return pltpu.make_async_remote_copy(
@@ -207,6 +223,26 @@
             dst_ref=nbuf.at[c, x, j, pc],
             send_sem=n_ss.at[c, 0],
             recv_sem=n_rs.at[c, j * 2 + pc],
+            device_id=dev(cc=1 - cc),
+            device_id_type=MESH,
+        )
+
+    def last_copy(dx, dy):
+        return pltpu.make_async_remote_copy(
+            src_ref=own_rows.at[LAST],
+            dst_ref=nbuf.at[LAST, x, y_lo, cc],
+            send_sem=last_ss.at[dx, dy],
+            recv_sem=last_rs.at[x, y_lo * 2 + cc],
+            device_id=dev(x=(x + dx) % 4, y=(y + dy) % 4, cc=y_hi),
+            device_id_type=MESH,
+        )
+
+    def last_arrival(e, j, pc):
+        return pltpu.make_async_remote_copy(
+            src_ref=own_rows.at[LAST],
+            dst_ref=nbuf.at[LAST, (x + e) % 4, j, pc],
+            send_sem=last_ss.at[0, 0],
+            recv_sem=last_rs.at[(x + e) % 4, j * 2 + pc],
             device_id=dev(cc=1 - cc),
             device_id_type=MESH,
         )
@@ -279,13 +315,9 @@
         psend[2 * h, :, zb] = block[:, :, :128]
         psend[2 * h + 1, :, zb] = block[:, :, 128:]
 
-    def send_y(c):
-        for d in (2, 1, 3):
-            y_copy(c, d).start()
-
-    def send_y_part(c, zb):
-        for d in (2, 1, 3):
-            y_part(c, d, zb).start()
+    def send_y(c, begin=0, end=4):
+        for copy in y_copies(c)[begin:end]:
+            copy().start()
 
     def make_weights():
         for load in small_loads:
@@ -303,11 +335,24 @@
             for c in range(CHUNKS):
                 wbuf[x, cc, c, k : k + 1, :] = weight[:, c * 128 : (c + 1) * 128]
 
+    def stage_pass(c):
+        up, _, down, _, up_next, down_next = y_copies(c)
+        low, high = pl.ds(0, 2), pl.ds(2, 2)
+        up().wait_recv()
+        total = passing[c, 0].astype(F32) + psend[c, (y + 1) % 4, low].astype(F32)
+        passed_on[c, 0] = total.astype(BF16)
+        up_next().start()
+        down().wait_recv()
+        total = passing[c, 1].astype(F32) + psend[c, (y + 3) % 4, high].astype(F32)
+        passed_on[c, 1] = total.astype(BF16)
+        down_next().start()
+
     def stage_y(c):
-        for d in range(1, 4):
-            y_copy(c, d).wait_recv()
+        copies = y_copies(c)
+        for i in (0, 1, 2) if c == LAST else (1, 3, 4, 5):
+            copies[i]().wait_recv()
         total = psend[c, y].astype(F32)
-        for d in range(3):
+        for d in range(3 if c == LAST else 2):
             total += yrecv[c, d].astype(F32)
         zsend[c] = total.astype(BF16)
         for d in (2, 1, 3):
@@ -330,31 +375,45 @@
         def _():
             nbuf[c, x, y_lo, cc] = own
 
-        for d in (2, 1, 3):
-            n_copy(c, d).start()
-
-        @pl.when(jnp.logical_not(own_n))
-        def _():
-            n_copy(c, 0).start()
-
-        for d in (2, 1, 3):
-            m_copy(c, d).start()
+        if c == LAST:
+            for d in (2, 1, 3):
+                m_copy(c, d).start()
+            for dx in (2, 1, 3, 0):
+                for dy in (2, 1, 3):
+                    last_copy(dx, dy).start()
+                if dx:
+                    last_copy(dx, 0).start()
+
+            @pl.when(jnp.logical_not(own_n))
+            def _():
+                last_copy(0, 0).start()
+        else:
+            for d in (2, 1, 3):
+                n_copy(c, d).start()
+
+            @pl.when(jnp.logical_not(own_n))
+            def _():
+                n_copy(c, 0).start()
+
+            for d in (2, 1, 3):
+                m_copy(c, d).start()
 
         @pl.when(jnp.logical_not(own_m))
         def _():
             m_copy(c, 0).start()
 
     def stage_relay(c):
-        for j in range(2):
-            for pc in range(2):
-                mine = jnp.logical_and(own_n, jnp.logical_and(y_lo == j, cc == pc))
-
-                @pl.when(jnp.logical_not(mine))
-                def _():
-                    n_arrival(c, j, pc).wait_recv()
-
-        for d in (2, 1, 3):
-            nx_copy(c, d).start()
+        if c < LAST:
+            for j in range(2):
+                for pc in range(2):
+                    mine = jnp.logical_and(own_n, jnp.logical_and(y_lo == j, cc == pc))
+
+                    @pl.when(jnp.logical_not(mine))
+                    def _():
+                        n_arrival(c, j, pc).wait_recv()
+
+            for d in (2, 1, 3):
+                nx_copy(c, d).start()
 
         @pl.when(jnp.logical_not(own_m))
         def _():
@@ -379,8 +438,20 @@
             ],
             axis=1,
         )
-        for d in range(1, 4):
-            nx_copy(c, d).wait_recv()
+        if c < LAST:
+            for d in range(1, 4):
+                nx_copy(c, d).wait_recv()
+        else:
+            for j in range(2):
+                for pc in range(2):
+                    mine = jnp.logical_and(own_n, jnp.logical_and(y_lo == j, cc == pc))
+
+                    @pl.when(jnp.logical_not(mine))
+                    def _():
+                        last_arrival(0, j, pc).wait_recv()
+
+                    for e in range(1, 4):
+                        last_arrival(e, j, pc).wait_recv()
         right = jnp.concatenate(
             [nbuf[c, xs, :, pc].reshape(128, 128) for xs, pc in groups], axis=1
         )
@@ -405,18 +476,15 @@
             f_copy(j).start()
 
     pp_load(0).wait()
-    basis_load(0).wait()
-    project_rows(0, 0)
-    pl.semaphore_wait(barrier, expected)
-    send_y_part(0, 0)
-
-    def first_rows(zb, carry):
+    for zb in range(2):
         basis_load(zb).wait()
         project_rows(0, zb)
-        send_y_part(0, zb)
-        return carry
-
-    lax.fori_loop(1, 4, first_rows, 0)
+    pl.semaphore_wait(barrier, expected)
+    send_y(0, 0, 2)
+    for zb in range(2, 4):
+        basis_load(zb).wait()
+        project_rows(0, zb)
+    send_y(0, 2, 4)
     send_y(1)
     pp_load(1).wait()
 
@@ -425,14 +493,18 @@
         return carry
 
     lax.fori_loop(0, 4, second_rows, 0)
+    stage_pass(0)
     send_y(2)
+    stage_pass(1)
     send_y(3)
     make_weights()
     w_copy.start()
+    stage_y(0)
+    stage_pass(2)
     w_copy.wait_recv()
     for d in range(1, 4):
         wx_copy(d).start()
-    for t in range(CHUNKS + 3):
+    for t in range(1, CHUNKS + 3):
         if t < CHUNKS:
             stage_y(t)
         if 0 <= t - 1 < CHUNKS:
@@ -445,16 +517,21 @@
         send_tile(j)
 
     for c in range(CHUNKS):
+        for copy in y_copies(c):
+            copy().wait_send()
         for d in range(1, 4):
-            y_copy(c, d).wait_send()
             z_copy(c, d).wait_send()
             m_copy(c, d).wait_send()
-            n_copy(c, d).wait_send()
-            nx_copy(c, d).wait_send()
+            if c < LAST:
+                n_copy(c, d).wait_send()
+                nx_copy(c, d).wait_send()
 
         @pl.when(jnp.logical_not(own_n))
         def _():
-            n_copy(c, 0).wait_send()
+            if c < LAST:
+                n_copy(c, 0).wait_send()
+            else:
+                last_copy(0, 0).wait_send()
 
         @pl.when(jnp.logical_not(own_m))
         def _():
@@ -462,6 +539,10 @@
 
         relay(c).wait_send()
     w_copy.wait_send()
+    for dx in range(4):
+        for dy in range(4):
+            if dx or dy:
+                last_copy(dx, dy).wait_send()
     for d in range(1, 4):
         wx_copy(d).wait_send()
 
@@ -503,6 +584,8 @@
             pltpu.VMEM((4, 2048, 256), BF16),
             pltpu.VMEM((HALVES, 2048, 256), BF16),
             pltpu.VMEM((CHUNKS, 4, 4, 64, 128), BF16),
+            pltpu.VMEM((LAST, 2, 2, 64, 128), BF16),
+            pltpu.VMEM((LAST, 2, 2, 64, 128), BF16),
             pltpu.VMEM((CHUNKS, 3, 4, 64, 128), BF16),
             pltpu.VMEM((CHUNKS, 4, 64, 128), BF16),
             pltpu.VMEM((CHUNKS, 3, 64, 128), BF16),
@@ -515,14 +598,16 @@
             pltpu.VMEM((2, 8, 32, 128), BF16),
             dma((4,)),
             dma((HALVES,)),
-            dma((CHUNKS, 3)),
-            dma((CHUNKS, 3)),
+            dma((CHUNKS, 6)),
+            dma((CHUNKS, 6)),
             dma((CHUNKS, 3)),
             dma((CHUNKS, 3)),
             dma((CHUNKS, 4)),
             dma((CHUNKS, 4)),
             dma((CHUNKS, 4)),
             dma((CHUNKS, 4)),
+            dma((4, 4)),
+            dma((4, 4)),
             dma((CHUNKS, 3)),
             dma((CHUNKS, 3)),
             dma((CHUNKS,)),

time: 50.5 us -> 53.5 us (1.059)
  Pallas kernels: 48.7 us -> 51.7 us
    pallas_call x1, Pallas kernels: 48.7 us -> 51.7 us  [per_device(): pl.pallas_call(functools.partial(kernel, pairs_total), out_shape=jax.Shap...]
where the time goes in v4:
time: 53.5 us; the launch traced here: 53.4 us
  Pallas kernels  51.7 us (97%)
  local copies, waits for them, and re-layouts  1.67 us (3%)
    pallas_call x1, Pallas kernels, per_device(): pl.pallas_call(functools.partial(kernel, pairs_total), out_shape=jax.Shap...  51.7 us
    unnamed x1, local copies, waits for them, and re-layouts  1.67 us

profile of v4, /device:TPU:1, one launch (start us, length us, event | category | flops | bytes accessed | tf_op | source)
XLA Modules:
  0.0 53.4 jit_solution(16562200116649665551)
XLA Ops:
  0.0 51.7 %shard_map.73 = f32[8,64,64]{2,1,0:T(8,128)} custom-call(bf16[2048,512]{1,0:T(8,128)(2,1)} %pp_hbm.1, bf16[2048,1024]{1,0:T(8,128)(2,1)} %basis_hbm.1, f32[1,128]{1,0:T(1,128)} %bitcast.6, f32[1,128]{1,0:T(1,128)} %bitcast.7, f32[8]{0:T(128)} %freq_hbm.1, s32[1,512]{1,0:T(1,128)} %bitcast.4, s32[1,512]{1,0:T(1,128)} %bitcast.5), custom_call_target="tpu_custom_call" | custom-call | tf_op jit(solution)/shard_map/pallas_call | solution.py:572
  51.7 1.7 %copy.9 = f32[8,64,64]{2,1,0:T(8,128)} copy(f32[8,64,64]{2,1,0:T(8,128)} %shard_map.73) | data formatting | bytes 262144

commit v5 on v3

--- a/solution.py
+++ b/solution.py
@@ -11,6 +11,8 @@
 BF16 = jnp.bfloat16
 MESH = pl.DeviceIdType.MESH
 CHUNKS = 4
+CROSSED = 1
+HALF = 32
 HALVES = 2
 
 
@@ -36,9 +38,14 @@
     yrecv,
     zsend,
     zrecv,
+    crossed_z,
+    crossed_y,
+    crossed_mine,
     own_rows,
     mbuf,
-    nbuf,
+    n_low,
+    n_high,
+    over_x,
     wbuf,
     acc,
     fsend,
@@ -55,6 +62,10 @@
     n_rs,
     nx_ss,
     nx_rs,
+    xf_ss,
+    xf_rs,
+    xn_ss,
+    xn_rs,
     r_ss,
     r_rs,
     w_ss,
@@ -85,8 +96,9 @@
         )
 
     pp_load(0).start()
-    for zb in range(4):
-        basis_load(zb).start()
+    row_order = (2, 1, 3, 0)
+    for d in row_order:
+        basis_load((zh + d) % 4).start()
     pp_load(1).start()
     small_loads = [
         pltpu.make_async_copy(source, target, small_sem.at[i])
@@ -171,6 +183,26 @@
             device_id_type=MESH,
         )
 
+    def zc_copy(d):
+        return pltpu.make_async_remote_copy(
+            src_ref=psend.at[CROSSED, :, (zh + d) % 4],
+            dst_ref=crossed_z.at[d - 1],
+            send_sem=z_ss.at[CROSSED, d - 1],
+            recv_sem=z_rs.at[CROSSED, d - 1],
+            device_id=dev(zh=(zh + d) % 4),
+            device_id_type=MESH,
+        )
+
+    def yc_copy(d):
+        return pltpu.make_async_remote_copy(
+            src_ref=crossed_y.at[(y + d) % 4],
+            dst_ref=crossed_mine.at[d - 1],
+            send_sem=y_ss.at[CROSSED, d - 1],
+            recv_sem=y_rs.at[CROSSED, d - 1],
+            device_id=dev(y=(y + d) % 4),
+            device_id_type=MESH,
+        )
+
     def m_copy(c, d):
         return pltpu.make_async_remote_copy(
             src_ref=own_rows.at[c],
@@ -191,34 +223,72 @@
             device_id_type=MESH,
         )
 
+    low, high = pl.ds(0, HALF), pl.ds(HALF, HALF)
+
+    def remote(source, target, send_sem, recv_sem, device):
+        return pltpu.make_async_remote_copy(
+            src_ref=source,
+            dst_ref=target,
+            send_sem=send_sem,
+            recv_sem=recv_sem,
+            device_id=device,
+            device_id_type=MESH,
+        )
+
+    sibling = dev(cc=1 - cc)
+
     def n_copy(c, d):
-        return pltpu.make_async_remote_copy(
-            src_ref=own_rows.at[c],
-            dst_ref=nbuf.at[c, x, y_lo, cc],
-            send_sem=n_ss.at[c, d],
-            recv_sem=n_rs.at[c, y_lo * 2 + cc],
-            device_id=dev(y=(y + d) % 4, cc=y_hi),
-            device_id_type=MESH,
+        return remote(
+            own_rows.at[c, low],
+            n_low.at[c, x, y_lo, cc],
+            n_ss.at[c, d],
+            n_rs.at[c, y_lo * 2 + cc],
+            dev(y=(y + d) % 4, cc=y_hi),
         )
 
     def n_arrival(c, j, pc):
-        return pltpu.make_async_remote_copy(
-            src_ref=own_rows.at[c],
-            dst_ref=nbuf.at[c, x, j, pc],
-            send_sem=n_ss.at[c, 0],
-            recv_sem=n_rs.at[c, j * 2 + pc],
-            device_id=dev(cc=1 - cc),
-            device_id_type=MESH,
+        return remote(
+            own_rows.at[c, low],
+            n_low.at[c, x, j, pc],
+            n_ss.at[c, 0],
+            n_rs.at[c, j * 2 + pc],
+            sibling,
         )
 
     def nx_copy(c, d):
-        return pltpu.make_async_remote_copy(
-            src_ref=nbuf.at[c, x],
-            dst_ref=nbuf.at[c, x],
-            send_sem=nx_ss.at[c, d - 1],
-            recv_sem=nx_rs.at[c, d - 1],
-            device_id=dev(x=(x + d) % 4),
-            device_id_type=MESH,
+        return remote(
+            n_low.at[c, x],
+            n_low.at[c, x],
+            nx_ss.at[c, d - 1],
+            nx_rs.at[c, d - 1],
+            dev(x=(x + d) % 4),
+        )
+
+    def xf_copy(c, d):
+        return remote(
+            own_rows.at[c, high],
+            over_x.at[c, x],
+            xf_ss.at[c, d - 1],
+            xf_rs.at[c, d - 1],
+            dev(x=(x + d) % 4),
+        )
+
+    def xn_copy(c, d):
+        return remote(
+            over_x.at[c],
+            n_high.at[c, y_lo, cc],
+            xn_ss.at[c, d],
+            xn_rs.at[c, y_lo * 2 + cc],
+            dev(y=(y + d) % 4, cc=y_hi),
+        )
+
+    def xn_arrival(c, j, pc):
+        return remote(
+            over_x.at[c],
+            n_high.at[c, j, pc],
+            xn_ss.at[c, 0],
+            xn_rs.at[c, j * 2 + pc],
+            sibling,
         )
 
     def relay(c):
@@ -319,6 +389,27 @@
         total = zsend[c, zh].astype(F32)
         for d in range(3):
             total += zrecv[c, d].astype(F32)
+        share(c, total)
+
+    def stage_crossed_z():
+        for d in range(1, 4):
+            zc_copy(d).wait_recv()
+        total = psend[CROSSED, :, zh].astype(F32)
+        for d in range(3):
+            total += crossed_z[d].astype(F32)
+        crossed_y[...] = total.astype(BF16)
+        for d in (2, 1, 3):
+            yc_copy(d).start()
+
+    def stage_crossed_y():
+        for d in range(1, 4):
+            yc_copy(d).wait_recv()
+        total = crossed_y[y].astype(F32)
+        for d in range(3):
+            total += crossed_mine[d].astype(F32)
+        share(CROSSED, total)
+
+    def share(c, total):
         own = total.astype(BF16)
         own_rows[c] = own
 
@@ -328,10 +419,12 @@
 
         @pl.when(own_n)
         def _():
-            nbuf[c, x, y_lo, cc] = own
-
+            n_low[c, x, y_lo, cc] = own[:HALF]
+
+        over_x[c, x] = own[HALF:]
         for d in (2, 1, 3):
             n_copy(c, d).start()
+            xf_copy(c, d).start()
 
         @pl.when(jnp.logical_not(own_n))
         def _():
@@ -344,18 +437,33 @@
         def _():
             m_copy(c, 0).start()
 
-    def stage_relay(c):
+    def each_foreign(body):
         for j in range(2):
             for pc in range(2):
                 mine = jnp.logical_and(own_n, jnp.logical_and(y_lo == j, cc == pc))
 
                 @pl.when(jnp.logical_not(mine))
                 def _():
-                    n_arrival(c, j, pc).wait_recv()
-
+                    body(j, pc)
+
+    def stage_relay(c):
+        each_foreign(lambda j, pc: n_arrival(c, j, pc).wait_recv())
         for d in (2, 1, 3):
             nx_copy(c, d).start()
-
+        for d in range(1, 4):
+            xf_copy(c, d).wait_recv()
+        for d in (2, 1, 3):
+            xn_copy(c, d).start()
+
+        @pl.when(own_n)
+        def _():
+            n_high[c, y_lo, cc] = over_x[c]
+
+        @pl.when(jnp.logical_not(own_n))
+        def _():
+            xn_copy(c, 0).start()
+
+    def stage_m(c):
         @pl.when(jnp.logical_not(own_m))
         def _():
             m_arrival(c, 0).wait_recv()
@@ -381,8 +489,20 @@
         )
         for d in range(1, 4):
             nx_copy(c, d).wait_recv()
+        each_foreign(lambda j, pc: xn_arrival(c, j, pc).wait_recv())
         right = jnp.concatenate(
-            [nbuf[c, xs, :, pc].reshape(128, 128) for xs, pc in groups], axis=1
+            [
+                jnp.concatenate(
+                    [
+                        part
+                        for j in range(2)
+                        for part in (n_low[c, xs, j, pc], n_high[c, j, pc, xs])
+                    ],
+                    axis=0,
+                )
+                for xs, pc in groups
+            ],
+            axis=1,
         )
         part = lax.dot_general(left, right, (((1,), (1,)), ((), ())), preferred_element_type=F32)
         if c == 0:
@@ -405,19 +525,15 @@
             f_copy(j).start()
 
     pp_load(0).wait()
-    basis_load(0).wait()
-    project_rows(0, 0)
-    pl.semaphore_wait(barrier, expected)
-    send_y_part(0, 0)
-
-    def first_rows(zb, carry):
+    for i, d in enumerate(row_order):
+        zb = (zh + d) % 4
         basis_load(zb).wait()
         project_rows(0, zb)
+        if i == 0:
+            pl.semaphore_wait(barrier, expected)
+        if d:
+            zc_copy(d).start()
         send_y_part(0, zb)
-        return carry
-
-    lax.fori_loop(1, 4, first_rows, 0)
-    send_y(1)
     pp_load(1).wait()
 
     def second_rows(zb, carry):
@@ -429,32 +545,50 @@
     send_y(3)
     make_weights()
     w_copy.start()
+    stage_y(0)
     w_copy.wait_recv()
     for d in range(1, 4):
         wx_copy(d).start()
-    for t in range(CHUNKS + 3):
-        if t < CHUNKS:
-            stage_y(t)
-        if 0 <= t - 1 < CHUNKS:
-            stage_z(t - 1)
-        if 0 <= t - 2 < CHUNKS:
-            stage_relay(t - 2)
-        if 0 <= t - 3 < CHUNKS:
-            stage_response(t - 3)
+    stage_crossed_z()
+    stage_y(2)
+    stage_z(0)
+    stage_y(3)
+    stage_crossed_y()
+    stage_z(2)
+    stage_relay(0)
+    stage_relay(1)
+    stage_m(0)
+    stage_z(3)
+    stage_relay(2)
+    stage_response(0)
+    stage_m(1)
+    stage_relay(3)
+    stage_response(1)
+    stage_m(2)
+    stage_response(2)
+    stage_m(3)
+    stage_response(3)
     for j in range(2):
         send_tile(j)
 
     for c in range(CHUNKS):
         for d in range(1, 4):
-            y_copy(c, d).wait_send()
-            z_copy(c, d).wait_send()
+            if c == CROSSED:
+                zc_copy(d).wait_send()
+                yc_copy(d).wait_send()
+            else:
+                y_copy(c, d).wait_send()
+                z_copy(c, d).wait_send()
             m_copy(c, d).wait_send()
             n_copy(c, d).wait_send()
             nx_copy(c, d).wait_send()
+            xf_copy(c, d).wait_send()
+            xn_copy(c, d).wait_send()
 
         @pl.when(jnp.logical_not(own_n))
         def _():
             n_copy(c, 0).wait_send()
+            xn_copy(c, 0).wait_send()
 
         @pl.when(jnp.logical_not(own_m))
         def _():
@@ -506,9 +640,14 @@
             pltpu.VMEM((CHUNKS, 3, 4, 64, 128), BF16),
             pltpu.VMEM((CHUNKS, 4, 64, 128), BF16),
             pltpu.VMEM((CHUNKS, 3, 64, 128), BF16),
+            pltpu.VMEM((3, 4, 64, 128), BF16),
+            pltpu.VMEM((4, 64, 128), BF16),
+            pltpu.VMEM((3, 64, 128), BF16),
             pltpu.VMEM((CHUNKS, 64, 128), BF16),
             pltpu.VMEM((CHUNKS, 2, 4, 64, 128), BF16),
-            pltpu.VMEM((CHUNKS, 4, 2, 2, 64, 128), BF16),
+            pltpu.VMEM((CHUNKS, 4, 2, 2, HALF, 128), BF16),
+            pltpu.VMEM((CHUNKS, 2, 2, 4, HALF, 128), BF16),
+            pltpu.VMEM((CHUNKS, 4, HALF, 128), BF16),
             pltpu.VMEM((4, 2, CHUNKS, 8, 128), F32),
             pltpu.VMEM((512, 128), F32),
             pltpu.VMEM((2, 8, 32, 128), BF16),
@@ -525,6 +664,10 @@
             dma((CHUNKS, 4)),
             dma((CHUNKS, 3)),
             dma((CHUNKS, 3)),
+            dma((CHUNKS, 3)),
+            dma((CHUNKS, 3)),
+            dma((CHUNKS, 4)),
+            dma((CHUNKS, 4)),
             dma((CHUNKS,)),
             dma((CHUNKS,)),
             dma(()),

time: 50.5 us -> 46.5 us (0.921)
  Pallas kernels: 48.7 us -> 44.7 us
    pallas_call x1, Pallas kernels: 48.7 us -> 44.7 us  [per_device(): pl.pallas_call(functools.partial(kernel, pairs_total), out_shape=jax.Shap...]
where the time goes in v5:
time: 46.5 us; the launch traced here: 46.4 us
  Pallas kernels  44.7 us (96%)
  local copies, waits for them, and re-layouts  1.67 us (4%)
    pallas_call x1, Pallas kernels, per_device(): pl.pallas_call(functools.partial(kernel, pairs_total), out_shape=jax.Shap...  44.7 us
    unnamed x1, local copies, waits for them, and re-layouts  1.67 us

profile of v5, /device:TPU:1, one launch (start us, length us, event | category | flops | bytes accessed | tf_op | source)
XLA Modules:
  0.0 46.4 jit_solution(5371945811536510564)
XLA Ops:
  0.0 44.7 %shard_map.73 = f32[8,64,64]{2,1,0:T(8,128)} custom-call(bf16[2048,512]{1,0:T(8,128)(2,1)} %pp_hbm.1, bf16[2048,1024]{1,0:T(8,128)(2,1)} %basis_hbm.1, f32[1,128]{1,0:T(1,128)} %bitcast.6, f32[1,128]{1,0:T(1,128)} %bitcast.7, f32[8]{0:T(128)} %freq_hbm.1, s32[1,512]{1,0:T(1,128)} %bitcast.4, s32[1,512]{1,0:T(1,128)} %bitcast.5), custom_call_target="tpu_custom_call" | custom-call | tf_op jit(solution)/shard_map/pallas_call | solution.py:625
  44.7 1.7 %copy.9 = f32[8,64,64]{2,1,0:T(8,128)} copy(f32[8,64,64]{2,1,0:T(8,128)} %shard_map.73) | data formatting | bytes 262144

commit v6 on v5

--- a/solution.py
+++ b/solution.py
@@ -32,6 +32,7 @@
     vidx_ref,
     cidx_ref,
     small_sem,
+    ready_sem,
     basis_v,
     pp_v,
     psend,
@@ -128,30 +129,8 @@
         greet(dev(zh=(zh + 4 - d) % 4))
         greet(dev(x=(x + 4 - d) % 4))
     greet(dev(cc=1 - cc))
-    for e in range(4):
-        source = dev(x=(x + e) % 4, zh=x)
-        if e == 0:
-
-            @pl.when(jnp.logical_not(own_m))
-            def _():
-                greet(source)
-        else:
-            greet(source)
-    for j in range(2):
-        for pc in range(2):
-            mine = jnp.logical_and(own_n, jnp.logical_and(y_lo == j, cc == pc))
-
-            @pl.when(jnp.logical_not(mine))
-            def _():
-                greet(dev(y=2 * cc + j, cc=pc))
-
-    greet(dev(zl=1 - zl, y=2 * zl + cc, cc=y_hi))
-
-    @pl.when(jnp.logical_not(own_c))
-    def _():
-        greet(dev(y=2 * zl + cc, cc=y_hi))
-
-    expected = 20 - jnp.where(own_m, 1, 0) - jnp.where(own_n, 1, 0) - jnp.where(own_c, 1, 0)
+    greet(dev(zl=1 - zl))
+    expected = 11
 
     def y_copy(c, d):
         return pltpu.make_async_remote_copy(
@@ -320,25 +299,21 @@
         device_id_type=MESH,
     )
 
-    def f_copy(j):
+    def f_copy(j, q):
         slot = (y_hi + zl) % 2
-        return pltpu.make_async_remote_copy(
-            src_ref=fsend.at[j],
-            dst_ref=frecv.at[slot],
-            send_sem=f_ss.at[j],
-            recv_sem=f_rs.at[slot],
-            device_id=dev(y=2 * cc + j, zl=y_hi, cc=y_lo),
-            device_id_type=MESH,
-        )
-
-    def f_arrival(slot):
-        return pltpu.make_async_remote_copy(
-            src_ref=fsend.at[0],
-            dst_ref=frecv.at[slot],
-            send_sem=f_ss.at[0],
-            recv_sem=f_rs.at[slot],
-            device_id=dev(cc=1 - cc),
-            device_id_type=MESH,
+        ks = pl.ds(q * 4, 4)
+        return remote(
+            fsend.at[j, ks],
+            frecv.at[slot, ks],
+            f_ss.at[j, q],
+            f_rs.at[slot, q],
+            dev(y=2 * cc + j, zl=y_hi, cc=y_lo),
+        )
+
+    def f_arrival(slot, q):
+        ks = pl.ds(q * 4, 4)
+        return remote(
+            fsend.at[0, ks], frecv.at[slot, ks], f_ss.at[0, q], f_rs.at[slot, q], sibling
         )
 
     def project_rows(h, zb):
@@ -410,6 +385,8 @@
         share(CROSSED, total)
 
     def share(c, total):
+        if c == 0:
+            pl.semaphore_wait(ready_sem, 6)
         own = total.astype(BF16)
         own_rows[c] = own
 
@@ -504,25 +481,39 @@
             ],
             axis=1,
         )
-        part = lax.dot_general(left, right, (((1,), (1,)), ((), ())), preferred_element_type=F32)
-        if c == 0:
-            acc[...] = part
+        if c < CHUNKS - 1:
+            part = lax.dot_general(
+                left, right, (((1,), (1,)), ((), ())), preferred_element_type=F32
+            )
+            if c == 0:
+                acc[...] = part
+            else:
+                acc[...] += part
         else:
-            acc[...] += part
-
-    def send_tile(j):
-        rows = acc[...].reshape(8, 64, 128)[:, :, j * 64 : (j + 1) * 64]
-        tile = jnp.concatenate([rows[:, :32], rows[:, 32:]], axis=2).astype(BF16)
-        fsend[j] = tile
-        mine = jnp.logical_and(own_c, y_lo == j)
-
-        @pl.when(mine)
-        def _():
-            frecv[0] = tile
-
-        @pl.when(jnp.logical_not(mine))
-        def _():
-            f_copy(j).start()
+            for q in range(2):
+                part = lax.dot_general(
+                    left[q * 256 : (q + 1) * 256],
+                    right,
+                    (((1,), (1,)), ((), ())),
+                    preferred_element_type=F32,
+                )
+                send_tiles(q, acc[q * 256 : (q + 1) * 256] + part)
+
+    def send_tiles(q, total):
+        ks = pl.ds(q * 4, 4)
+        for j in range(2):
+            rows = total.reshape(4, 64, 128)[:, :, j * 64 : (j + 1) * 64]
+            tile = jnp.concatenate([rows[:, :32], rows[:, 32:]], axis=2).astype(BF16)
+            fsend[j, ks] = tile
+            mine = jnp.logical_and(own_c, y_lo == j)
+
+            @pl.when(mine)
+            def _():
+                frecv[0, ks] = tile
+
+            @pl.when(jnp.logical_not(mine))
+            def _():
+                f_copy(j, q).start()
 
     pp_load(0).wait()
     for i, d in enumerate(row_order):
@@ -531,6 +522,11 @@
         project_rows(0, zb)
         if i == 0:
             pl.semaphore_wait(barrier, expected)
+            for step in range(1, 4):
+                for peer in (dev(y=(y + step) % 4), dev(zh=(zh + step) % 4)):
+                    pl.semaphore_signal(
+                        ready_sem, inc=1, device_id=peer, device_id_type=MESH
+                    )
         if d:
             zc_copy(d).start()
         send_y_part(0, zb)
@@ -540,7 +536,7 @@
         project_rows(1, zb)
         return carry
 
-    lax.fori_loop(0, 4, second_rows, 0)
+    lax.fori_loop(0, 4, second_rows, 0, unroll=True)
     send_y(2)
     send_y(3)
     make_weights()
@@ -568,9 +564,6 @@
     stage_response(2)
     stage_m(3)
     stage_response(3)
-    for j in range(2):
-        send_tile(j)
-
     for c in range(CHUNKS):
         for d in range(1, 4):
             if c == CROSSED:
@@ -599,20 +592,24 @@
     for d in range(1, 4):
         wx_copy(d).wait_send()
 
-    @pl.when(jnp.logical_not(own_c))
-    def _():
-        f_arrival(0).wait_recv()
-
-    f_arrival(1).wait_recv()
-    total = frecv[0].astype(F32) + frecv[1].astype(F32)
-    rows = jnp.concatenate([total[:, :, :64], total[:, :, 64:]], axis=1)
-    out_ref[...] = jnp.swapaxes(rows, 1, 2)
+    for q in range(2):
+        ks = pl.ds(q * 4, 4)
+
+        @pl.when(jnp.logical_not(own_c))
+        def _():
+            f_arrival(0, q).wait_recv()
+
+        f_arrival(1, q).wait_recv()
+        total = frecv[0, ks].astype(F32) + frecv[1, ks].astype(F32)
+        rows = jnp.concatenate([total[:, :, :64], total[:, :, 64:]], axis=1)
+        out_ref[ks] = jnp.swapaxes(rows, 1, 2)
     for j in range(2):
         mine = jnp.logical_and(own_c, y_lo == j)
 
         @pl.when(jnp.logical_not(mine))
         def _():
-            f_copy(j).wait_send()
+            for q in range(2):
+                f_copy(j, q).wait_send()
 
 
 def per_device(
@@ -634,6 +631,7 @@
             pltpu.VMEM((1, 512), jnp.int32),
             pltpu.VMEM((1, 512), jnp.int32),
             dma((5,)),
+            pltpu.SemaphoreType.REGULAR,
             pltpu.VMEM((4, 2048, 256), BF16),
             pltpu.VMEM((HALVES, 2048, 256), BF16),
             pltpu.VMEM((CHUNKS, 4, 4, 64, 128), BF16),
@@ -674,8 +672,8 @@
             dma(()),
             dma((3,)),
             dma((3,)),
-            dma((2,)),
-            dma((2,)),
+            dma((2, 2)),
+            dma((2, 2)),
         ],
         compiler_params=pltpu.CompilerParams(
             collective_id=0, has_side_effects=True, vmem_limit_bytes=56 * 2**20

time: 46.5 us -> 45.6 us (0.981)
  Pallas kernels: 44.7 us -> 43.8 us
    pallas_call x1, Pallas kernels: 44.7 us -> 43.8 us  [per_device(): pl.pallas_call(functools.partial(kernel, pairs_total), out_shape=jax.Shap...]
where the time goes in v6:
time: 45.6 us; the launch traced here: 45.5 us
  Pallas kernels  43.8 us (96%)
  local copies, waits for them, and re-layouts  1.67 us (4%)
    pallas_call x1, Pallas kernels, per_device(): pl.pallas_call(functools.partial(kernel, pairs_total), out_shape=jax.Shap...  43.8 us
    unnamed x1, local copies, waits for them, and re-layouts  1.67 us

profile of v6, /device:TPU:1, one launch (start us, length us, event | category | flops | bytes accessed | tf_op | source)
XLA Modules:
  0.0 45.5 jit_solution(7360188968577777332)
XLA Ops:
  0.0 43.8 %shard_map.73 = f32[8,64,64]{2,1,0:T(8,128)} custom-call(bf16[2048,512]{1,0:T(8,128)(2,1)} %pp_hbm.1, bf16[2048,1024]{1,0:T(8,128)(2,1)} %basis_hbm.1, f32[1,128]{1,0:T(1,128)} %bitcast.6, f32[1,128]{1,0:T(1,128)} %bitcast.7, f32[8]{0:T(128)} %freq_hbm.1, s32[1,512]{1,0:T(1,128)} %bitcast.4, s32[1,512]{1,0:T(1,128)} %bitcast.5), custom_call_target="tpu_custom_call" | custom-call | tf_op jit(solution)/shard_map/pallas_call | solution.py:622
  43.8 1.7 %copy.9 = f32[8,64,64]{2,1,0:T(8,128)} copy(f32[8,64,64]{2,1,0:T(8,128)} %shard_map.73) | data formatting | bytes 262144

commit v7 on v6

--- a/solution.py
+++ b/solution.py
@@ -527,9 +527,9 @@
                     pl.semaphore_signal(
                         ready_sem, inc=1, device_id=peer, device_id_type=MESH
                     )
+        send_y_part(0, zb)
         if d:
             zc_copy(d).start()
-        send_y_part(0, zb)
     pp_load(1).wait()
 
     def second_rows(zb, carry):
@@ -539,9 +539,9 @@
     lax.fori_loop(0, 4, second_rows, 0, unroll=True)
     send_y(2)
     send_y(3)
+    stage_y(0)
     make_weights()
     w_copy.start()
-    stage_y(0)
     w_copy.wait_recv()
     for d in range(1, 4):
         wx_copy(d).start()

time: 45.6 us -> 45.7 us (level)
  no operation moved by 1% of the time
where the time goes in v7:
time: 45.7 us; the launch traced here: 45.6 us
  Pallas kernels  43.9 us (96%)
  local copies, waits for them, and re-layouts  1.67 us (4%)
    pallas_call x1, Pallas kernels, per_device(): pl.pallas_call(functools.partial(kernel, pairs_total), out_shape=jax.Shap...  43.9 us
    unnamed x1, local copies, waits for them, and re-layouts  1.67 us

profile of v7, /device:TPU:1, one launch (start us, length us, event | category | flops | bytes accessed | tf_op | source)
XLA Modules:
  0.0 45.6 jit_solution(3952642309929607857)
XLA Ops:
  0.0 43.9 %shard_map.73 = f32[8,64,64]{2,1,0:T(8,128)} custom-call(bf16[2048,512]{1,0:T(8,128)(2,1)} %pp_hbm.1, bf16[2048,1024]{1,0:T(8,128)(2,1)} %basis_hbm.1, f32[1,128]{1,0:T(1,128)} %bitcast.6, f32[1,128]{1,0:T(1,128)} %bitcast.7, f32[8]{0:T(128)} %freq_hbm.1, s32[1,512]{1,0:T(1,128)} %bitcast.4, s32[1,512]{1,0:T(1,128)} %bitcast.5), custom_call_target="tpu_custom_call" | custom-call | tf_op jit(solution)/shard_map/pallas_call | solution.py:622
  43.9 1.7 %copy.9 = f32[8,64,64]{2,1,0:T(8,128)} copy(f32[8,64,64]{2,1,0:T(8,128)} %shard_map.73) | data formatting | bytes 262144

commit v8 on v6

--- a/solution.py
+++ b/solution.py
@@ -534,10 +534,10 @@
 
     def second_rows(zb, carry):
         project_rows(1, zb)
+        send_y_part(2, zb)
         return carry
 
     lax.fori_loop(0, 4, second_rows, 0, unroll=True)
-    send_y(2)
     send_y(3)
     make_weights()
     w_copy.start()

time: 45.6 us -> 45.8 us (level)
  no operation moved by 1% of the time
where the time goes in v8:
time: 45.8 us; the launch traced here: 45.7 us
  Pallas kernels  44 us (96%)
  local copies, waits for them, and re-layouts  1.67 us (4%)
    pallas_call x1, Pallas kernels, per_device(): pl.pallas_call(functools.partial(kernel, pairs_total), out_shape=jax.Shap...  44 us
    unnamed x1, local copies, waits for them, and re-layouts  1.67 us

profile of v8, /device:TPU:1, one launch (start us, length us, event | category | flops | bytes accessed | tf_op | source)
XLA Modules:
  0.0 45.7 jit_solution(3663737757610100324)
XLA Ops:
  0.0 44.0 %shard_map.73 = f32[8,64,64]{2,1,0:T(8,128)} custom-call(bf16[2048,512]{1,0:T(8,128)(2,1)} %pp_hbm.1, bf16[2048,1024]{1,0:T(8,128)(2,1)} %basis_hbm.1, f32[1,128]{1,0:T(1,128)} %bitcast.6, f32[1,128]{1,0:T(1,128)} %bitcast.7, f32[8]{0:T(128)} %freq_hbm.1, s32[1,512]{1,0:T(1,128)} %bitcast.4, s32[1,512]{1,0:T(1,128)} %bitcast.5), custom_call_target="tpu_custom_call" | custom-call | tf_op jit(solution)/shard_map/pallas_call | solution.py:622
  44.0 1.7 %copy.9 = f32[8,64,64]{2,1,0:T(8,128)} copy(f32[8,64,64]{2,1,0:T(8,128)} %shard_map.73) | data formatting | bytes 262144
